TPU v7x, 32 devices: a whole 2x2x4 slice. The times are simulated.
32 devices in a mesh: tile: 8 (over y, x, core), member: 4 (over z).
Axes of the slice: x: 2, y: 2, z: 4, core: 2. Of those that a mesh axis runs over, the one named last changes fastest.
Arguments:
- residual_in: float32 [64, 128, 512], P(None, 'tile', 'member'), may hold values from -6 to 6
- members: bfloat16 [8, 64, 128, 512], P('member', None, 'tile'), may hold values from -6 to 6
- wind_x: float32 [64], replicated, may hold values from 0.05 to 0.25
- wind_y: float32 [64], replicated, may hold values from 0.05 to 0.25
Outputs:
- analysis: float32 [64, 128, 512], P(None, 'tile', 'member')
- residual: float32 [64, 128, 512], P(None, 'tile', 'member')
All inputs are finite; a program needn't handle non-finite values.
Results may differ from a plain program's by a relative error of at most 0.006.
Values may be sent and summed in bfloat16 or wider, within the bound.
No kernel may reach another device: no remote copies, remote signals or barrier semaphores. Data moves between devices by JAX's collectives and lax.ppermute only.
A program may use at most 64 MiB of HBM per device.

v0:
```python
import functools

import jax
import jax.numpy as jnp
from jax import lax
from jax.experimental import pallas as pl
from jax.experimental.pallas import tpu as pltpu
from jax.sharding import PartitionSpec as P

ITERS = 2
MODEL_STEPS = 4
DIFFUSION = 0.1
RELAX = 0.5
REACH = 16
TAPER_TOTAL = sum(1.0 - (k / 17.0) ** 2 for k in range(-REACH, REACH + 1))
F32 = jnp.float32
BF16 = jnp.bfloat16
LANES = 128
SUB = 8
GROUP = LANES // (2 * MODEL_STEPS)

VMEM = pl.BlockSpec(memory_space=pltpu.VMEM)
SMEM = pl.BlockSpec(memory_space=pltpu.SMEM)
PARAMS = pltpu.CompilerParams(vmem_limit_bytes=48 * 1024 * 1024)


def call(body, out_shape, *args, in_specs=None, scratch=()):
    return pl.pallas_call(
        body,
        out_shape=out_shape,
        in_specs=in_specs or [VMEM] * len(args),
        out_specs=jax.tree.map(lambda _: VMEM, out_shape),
        scratch_shapes=scratch,
        compiler_params=PARAMS,
    )(*args)


def lane_iota(shape):
    return lax.broadcasted_iota(jnp.int32, shape, len(shape) - 1)


def sub_iota(shape):
    return lax.broadcasted_iota(jnp.int32, shape, len(shape) - 2)


def neighbor_of(place_ref, step):
    member, parts = place_ref[2], place_ref[3]
    return lax.rem(member + parts + step, parts)


def split_body(turns, place_ref, in_ref, *out_refs):
    own, planes, rows, cols = out_refs[0].shape
    levels = in_ref.shape[1]
    slot = lane_iota((rows, LANES)) // MODEL_STEPS

    def block(step):
        return pl.ds(pl.multiple_of(neighbor_of(place_ref, step) * cols, cols), cols)

    for r, out_ref in zip(turns, out_refs):
        before, here, after = block(r - 1), block(r), block(r + 1)
        for m in range(own):

            def step(g, carry):
                total = jnp.zeros((rows, LANES), F32)
                for k in range(GROUP):
                    level = g * GROUP + k
                    out_ref[m, level] = in_ref[m, level, :, here]
                    left = in_ref[m, level, :, before].astype(F32)
                    right = in_ref[m, level, :, after].astype(F32)
                    total = jnp.where(slot == k, pltpu.roll(left, MODEL_STEPS * (k + 1), 1), total)
                    total = jnp.where(slot == GROUP + k, pltpu.roll(right, MODEL_STEPS * (GROUP + k), 1), total)
                out_ref[m, levels + g] = total.astype(out_ref.dtype)
                return carry

            lax.fori_loop(0, levels // GROUP, step, 0)


def split_columns(place, members, parts, turns):
    own, levels, rows, ny = members.shape
    out = jax.ShapeDtypeStruct((own, levels + levels // GROUP, rows, ny // parts), members.dtype)
    return call(functools.partial(split_body, turns), (out,) * len(turns), place, members, in_specs=[SMEM, VMEM])


def third_tile(below, above, odd):
    upper = sub_iota((SUB, LANES)) < MODEL_STEPS
    if odd:
        return jnp.where(upper, pltpu.roll(below, MODEL_STEPS, 0), above)
    return jnp.where(upper, below, pltpu.roll(above, MODEL_STEPS, 0))


def pack_rows(ref, at, top_ref, bottom_ref):
    upper = sub_iota((SUB, LANES)) < MODEL_STEPS
    count, rows, _ = ref.shape
    for q in range(count // 2):
        top_ref[at + q] = jnp.where(upper, ref[2 * q, :SUB], pltpu.roll(ref[2 * q + 1, :SUB], MODEL_STEPS, 0))
        bottom_ref[at + q] = jnp.where(
            upper, pltpu.roll(ref[2 * q, rows - SUB :], MODEL_STEPS, 0), ref[2 * q + 1, rows - SUB :]
        )


def rows_body(x_ref, top_ref, bottom_ref):
    pack_rows(x_ref, 0, top_ref, bottom_ref)


def edge_rows(x):
    out = jax.ShapeDtypeStruct((x.shape[0] // 2, SUB, LANES), F32)
    return call(rows_body, (out, out), x)


def columns_edge_body(x_ref, above_ref, below_ref, first_ref, last_ref):
    levels, rows, cols = x_ref.shape
    slot = lane_iota((rows + SUB, LANES)) // MODEL_STEPS

    def step(g, carry):
        first = jnp.zeros((rows + SUB, LANES), F32)
        last = jnp.zeros((rows + SUB, LANES), F32)
        for k in range(GROUP):
            level = g * GROUP + k
            pair = g * (GROUP // 2) + k // 2
            x = jnp.concatenate([x_ref[level], third_tile(below_ref[pair], above_ref[pair], k % 2)], axis=0)
            last = jnp.where(slot == k, pltpu.roll(x, MODEL_STEPS * (k + 1), 1), last)
            first = jnp.where(slot == GROUP + k, pltpu.roll(x, MODEL_STEPS * (GROUP + k), 1), first)
        first_ref[g] = first
        last_ref[g] = last
        return carry

    lax.fori_loop(0, levels // GROUP, step, 0)


def edge_columns(x, above, below):
    levels, rows, cols = x.shape
    out = jax.ShapeDtypeStruct((levels // GROUP, rows + SUB, LANES), F32)
    return call(columns_edge_body, (out, out), x, above, below)


def shift(x, axis, step):
    count = lax.axis_size(axis)
    pairs = [(i, i + step) for i in range(count) if 0 <= i + step < count]
    return lax.ppermute(x, axis, pairs)


def sweep_block(level_pair, x_ref, sides_ref, above_ref, below_ref, wx_ref, wy_ref, mask):
    rows = x_ref.shape[1]
    lanes = lane_iota((rows + SUB, LANES))
    ext_rows = rows + SUB
    ext_cols = 2 * LANES
    above = above_ref[level_pair]
    below = below_ref[level_pair]
    results = []
    for odd in range(2):
        level = 2 * level_pair + odd
        k = level % GROUP
        packed = sides_ref[level // GROUP]
        side_right = pltpu.roll(packed, (LANES + LANES // 2 - MODEL_STEPS * k) % LANES, 1)
        side_left = pltpu.roll(packed, LANES - MODEL_STEPS * (k + 1), 1)
        side = jnp.where(lanes < MODEL_STEPS, side_right, side_left)
        center = jnp.concatenate([x_ref[level], third_tile(below, above, odd)], axis=0)
        field = jnp.concatenate([center, side], axis=1) * mask
        wx = wx_ref[level]
        wy = wy_ref[level]
        own = 1.0 - 4.0 * DIFFUSION - wx - wy
        ahead_x = DIFFUSION + wx
        ahead_y = DIFFUSION + wy
        for _ in range(MODEL_STEPS):
            field = (
                own * field
                + ahead_x * pltpu.roll(field, ext_rows - 1, 0)
                + ahead_y * pltpu.roll(field, ext_cols - 1, 1)
                + DIFFUSION * (pltpu.roll(field, 1, 0) + pltpu.roll(field, 1, 1))
            ) * mask
        results.append(field[:rows, :LANES])
    return results


def block_mask(place_ref, rows, cols):
    tile, tiles, member, parts = (place_ref[i] for i in range(4))
    shape = (rows + SUB, 2 * LANES)
    r = sub_iota(shape)
    c = lane_iota(shape)
    r = jnp.where(r < rows + MODEL_STEPS, r, r - rows - SUB)
    near = (c < cols + MODEL_STEPS) | (c >= 2 * LANES - MODEL_STEPS)
    c = jnp.where(c < cols + MODEL_STEPS, c, c - 2 * LANES)
    gr = r + tile * rows
    gc = c + member * cols
    inside = (gr >= 0) & (gr < tiles * rows) & (gc >= 0) & (gc < parts * cols) & near
    return jnp.where(inside, 1.0, 0.0).astype(F32)


def first_model_body(place_ref, wx_ref, wy_ref, x_ref, left_ref, right_ref, above_ref, below_ref, grad_ref, sides_ref):
    levels, rows, cols = x_ref.shape
    mask = block_mask(place_ref, rows, cols)
    sides_ref[...] = left_ref[...] + right_ref[...]

    def step(q, carry):
        for u in range(2):
            pair = 2 * q + u
            for odd, value in enumerate(
                sweep_block(pair, x_ref, sides_ref, above_ref, below_ref, wx_ref, wy_ref, mask)
            ):
                grad_ref[2 * pair + odd] = value
        return carry

    lax.fori_loop(0, levels // 4, step, 0)


def second_model_body(
    place_ref, wx_ref, wy_ref, x_ref, beside_ref, above_ref, below_ref, *refs
):
    *others, grad_ref, sides_ref = refs
    levels, rows, cols = x_ref.shape
    groups = beside_ref.shape[0]
    mask = block_mask(place_ref, rows, cols)
    for g in range(groups):
        at = (levels + g) // 2
        sides_ref[g, :rows] = beside_ref[g]
        sides_ref[g, rows:] = third_tile(below_ref[at], above_ref[at], g % 2)

    def step(q, carry):
        for u in range(2):
            pair = 2 * q + u
            for odd, value in enumerate(
                sweep_block(pair, x_ref, sides_ref, above_ref, below_ref, wx_ref, wy_ref, mask)
            ):
                grad_ref[2 * pair + odd] = value
        return carry

    lax.fori_loop(0, levels // 4, step, 0)
    project_body(place_ref, grad_ref, *others)


def project_body(place_ref, grad_ref, *refs):
    *member_refs, wide_ref, thin_ref = refs
    own, _, rows, cols = member_refs[0].shape
    count = len(member_refs) * own

    def step(q, carry):
        carry = list(carry)
        for u in range(2):
            g = grad_ref[2 * q + u]
            for m in range(count):
                carry[m] = carry[m] + member_refs[m // own][m % own, 2 * q + u].astype(F32) * g
        return tuple(carry)

    total = lax.fori_loop(0, grad_ref.shape[0] // 2, step, (jnp.zeros((rows, cols), F32),) * count)
    for m in range(count):
        at = neighbor_of(place_ref, -(m // own)) * own + m % own
        wide_ref[at] = total[m]
        thin_ref[at] = total[m].astype(BF16)


def taper(offset):
    k = offset.astype(F32)
    w = (1.0 - (k / 17.0) * (k / 17.0)) * (1.0 / TAPER_TOTAL)
    return jnp.where(jnp.abs(offset) <= REACH, w, 0.0)


def halves(x):
    high = x.astype(BF16)
    return high, (x - high.astype(F32)).astype(BF16)


def sharp_dot(a, b):
    ah, al = halves(a)
    bh, bl = halves(b)
    dot = functools.partial(jnp.dot, preferred_element_type=F32)
    return dot(ah, bh) + dot(al, bh) + dot(ah, bl)


def columns_body(left_ref, mid_ref, right_ref, wide_ref, thin_ref):
    count, rows, cols = mid_ref.shape
    wide = jnp.concatenate(
        [r[...].astype(F32).reshape(count * rows, cols) for r in (left_ref, mid_ref, right_ref)], axis=1
    )
    shape = (3 * cols, wide_ref.shape[0] // count * cols)
    lane = lane_iota(shape)
    beside = lane % MODEL_STEPS + jnp.where(lane < cols + LANES // 2, -MODEL_STEPS, cols)
    target = jnp.where(lane < cols, lane, beside)
    out = sharp_dot(wide, taper(sub_iota(shape) - cols - target))
    for i in range(shape[1] // cols):
        part = out[:, i * cols : (i + 1) * cols].reshape(count, rows, cols)
        wide_ref[i * count : (i + 1) * count] = part
        thin_ref[i * count : (i + 1) * count] = part.astype(BF16)


def smooth_rows(above_ref, mid_ref, below_ref):
    count, rows, cols = mid_ref.shape
    tall = jnp.concatenate(
        [
            jnp.concatenate([above_ref[m].astype(F32), mid_ref[m], below_ref[m].astype(F32)], axis=0)
            for m in range(count)
        ],
        axis=1,
    )
    shape = (rows, 3 * rows)
    out = sharp_dot(taper(lane_iota(shape) - sub_iota(shape) - rows), tall)
    return [out[:, m * cols : (m + 1) * cols] for m in range(count)]


def increments(place_ref, member_refs, local_ref, levels, emit):
    own = member_refs[0].shape[0]
    count = len(member_refs) * own
    local = [local_ref[neighbor_of(place_ref, -(m // own)) * own + m % own] for m in range(count)]

    def step(q, carry):
        for u in range(2):
            level = 2 * q + u
            total = member_refs[0][0, level].astype(F32) * local[0]
            for m in range(1, count):
                total = total + member_refs[m // own][m % own, level].astype(F32) * local[m]
            emit(level, total)
        return carry

    lax.fori_loop(0, levels // 2, step, 0)


def update_body(parts, place_ref, residual_ref, left_ref, right_ref, above_ref, mid_ref, below_ref, *refs):
    member_refs = refs[:parts]
    analysis_ref, out_ref, beside_ref, top_ref, bottom_ref, local_ref = refs[parts:]
    levels, rows, cols = residual_ref.shape
    own = member_refs[0].shape[0]
    count = parts * own
    for m, value in enumerate(smooth_rows(above_ref, mid_ref, below_ref)):
        local_ref[m] = value

    def emit(level, value):
        analysis_ref[level] = value
        out_ref[level] = residual_ref[level] - RELAX * value

    increments(place_ref, member_refs, local_ref, levels, emit)
    for g in range(levels // GROUP):
        total = jnp.zeros((rows, LANES), F32)
        for m in range(count):
            at = neighbor_of(place_ref, -(m // own)) * own + m % own
            total = total + member_refs[m // own][m % own, levels + g].astype(F32) * local_ref[count + at]
        beside_ref[g] = left_ref[g, :rows] + right_ref[g, :rows] - RELAX * total
    pack_rows(out_ref, 0, top_ref, bottom_ref)
    pack_rows(beside_ref, levels // 2, top_ref, bottom_ref)


def final_body(parts, place_ref, residual_ref, before_ref, above_ref, mid_ref, below_ref, *refs):
    member_refs = refs[:parts]
    analysis_ref, out_ref, local_ref = refs[parts:]
    for m, value in enumerate(smooth_rows(above_ref, mid_ref, below_ref)):
        local_ref[m] = value

    def emit(level, value):
        analysis_ref[level] = before_ref[level] + value
        out_ref[level] = residual_ref[level] - RELAX * value

    increments(place_ref, member_refs, local_ref, residual_ref.shape[0], emit)


def per_device(residual_in, members, wind_x, wind_y):
    levels, rows, cols = residual_in.shape
    tiles = lax.axis_size("tile")
    parts = lax.axis_size("member")
    place = jnp.stack([lax.axis_index("tile"), jnp.int32(tiles), lax.axis_index("member"), jnp.int32(parts)])
    count = members.shape[0] * parts
    groups = levels // GROUP

    def shape(*dims, kind=F32):
        return jax.ShapeDtypeStruct(dims, kind)

    def both(*dims):
        return shape(*dims), shape(*dims, kind=BF16)

    def turned(x, step):
        return lax.ppermute(x, "member", [(i, (i + step) % parts) for i in range(parts)])

    def smoothed(wide, thin, planes):
        wide, thin = call(
            columns_body, both(planes, rows, cols), shift(thin, "member", 1), wide, shift(thin, "member", -1)
        )
        return shift(thin, "tile", 1), wide, shift(thin, "tile", -1)

    like = shape(levels, rows, cols)
    sides = [pltpu.VMEM((groups, rows + SUB, LANES), F32)]

    far = parts // 2
    (soon,) = split_columns(place, members, parts, (far,))
    soon, residual_in = lax.optimization_barrier((soon, residual_in))
    blocks = {far: turned(soon, far)}
    top, bottom = edge_rows(residual_in)
    above, below = shift(bottom, "tile", 1), shift(top, "tile", -1)
    first, last = edge_columns(residual_in, above, below)
    left, right = shift(last, "member", 1), shift(first, "member", -1)
    members, first = lax.optimization_barrier((members, first))
    turns = [r for r in range(parts) if r != far]
    later = split_columns(place, members, parts, turns)
    later, left, right = lax.optimization_barrier((later, left, right))
    for r, block in zip(turns, later):
        blocks[r] = turned(block, r) if r else block
    blocks = [blocks[r] for r in range(parts)]
    grad = call(
        first_model_body, like,
        place, wind_x, wind_y, residual_in, left, right, above, below,
        in_specs=[SMEM] * 3 + [VMEM] * 5, scratch=sides,
    )
    wide, thin = call(
        project_body, both(count, rows, cols), place, grad, *blocks, in_specs=[SMEM] + [VMEM] * (1 + parts)
    )

    halo = shape((levels + groups) // 2, SUB, LANES)
    analysis, residual, beside, top, bottom = call(
        functools.partial(update_body, parts), (like, like, shape(groups, rows, LANES), halo, halo),
        place, residual_in, left, right, *smoothed(wide, thin, 2 * count), *blocks,
        in_specs=[SMEM] + [VMEM] * (6 + parts), scratch=[pltpu.VMEM((2 * count, rows, cols), F32)],
    )
    above, below = shift(bottom, "tile", 1), shift(top, "tile", -1)
    wide, thin = call(
        second_model_body, both(count, rows, cols),
        place, wind_x, wind_y, residual, beside, above, below, *blocks,
        in_specs=[SMEM] * 3 + [VMEM] * (4 + parts), scratch=[pltpu.VMEM((levels, rows, cols), F32)] + sides,
    )
    return call(
        functools.partial(final_body, parts), (like, like),
        place, residual, analysis, *smoothed(wide, thin, count), *blocks,
        in_specs=[SMEM] + [VMEM] * (5 + parts), scratch=[pltpu.VMEM((count, rows, cols), F32)],
    )


def solution(mesh):
    return jax.shard_map(
        per_device,
        mesh=mesh,
        in_specs=(P(None, "tile", "member"), P("member", None, "tile", None), P(), P()),
        out_specs=(P(None, "tile", "member"), P(None, "tile", "member")),
        check_vma=False,
    )
```

profile of v0, /device:TPU:20, one launch (start us, length us, event | category | flops | bytes accessed | tf_op | source)
XLA Modules:
  0.0 128.0 jit_solution(7451427356177161607)
XLA Ops:
  0.7 1.6 %copy-done.1 = bf16[2,64,16,512]{3,2,1,0:T(8,128)(2,1)S(1)} copy-done((bf16[2,64,16,512]{3,2,1,0:T(8,128)(2,1)S(1)}, bf16[2,64,16,512]{3,2,1,0:T(8,128)(2,1)}, u32[]{:S(2)}) %copy-start.1) | copy-done | bytes 2097176
  2.4 1.5 %shard_map.59 = bf16[2,68,16,128]{3,2,1,0:T(8,128)(2,1)S(1)} custom-call(s32[4]{0:T(128)S(1)} %pad_add_fusion.place_ref, bf16[2,64,16,512]{3,2,1,0:T(8,128)(2,1)S(1)} %copy-done.1), custom_call_target="tpu_custom_call" | custom-call | tf_op jit(solution)/shard_map/pallas_call | solution.py:28
  3.9 1.9 %collective-permute-start = (f32[32,8,128]{2,1,0:T(8,128)S(1)}, f32[32,8,128]{2,1,0:T(8,128)S(1)}, u32[]{:S(2)}, u32[]{:S(2)}) collective-permute-start(f32[32,8,128]{2,1,0:T(8,128)S(1)} %get-tuple-element.31), channel_id=1, source_target_pairs={{0,4},{4,8},{8,12},{12,16},{16,20},{20,24},{24,28},{1,5},{5,9},{9,... | collective-permute-start | bytes 393224 | tf_op jit(solution)/shard_map/ppermute | solution.py:139
  5.9 4.5 %collective-permute-start.1 = (f32[32,8,128]{2,1,0:T(8,128)S(1)}, f32[32,8,128]{2,1,0:T(8,128)S(1)}, u32[]{:S(2)}, u32[]{:S(2)}) collective-permute-start(f32[32,8,128]{2,1,0:T(8,128)S(1)} %get-tuple-element.32), channel_id=1, source_target_pairs={{4,0},{8,4},{12,8},{16,12},{20,16},{24,20},{28,24},{5,1},{9,5},{13... | collective-permute-start | bytes 393224 | tf_op jit(solution)/shard_map/ppermute | solution.py:139
  11.1 1.8 %collective-permute-done.1.below_ref = f32[32,8,128]{2,1,0:T(8,128)S(1)} collective-permute-done((f32[32,8,128]{2,1,0:T(8,128)S(1)}, f32[32,8,128]{2,1,0:T(8,128)S(1)}, u32[]{:S(2)}, u32[]{:S(2)}) %collective-permute-start.1) | collective-permute-done | bytes 131104 | tf_op jit(solution)/shard_map/ppermute | solution.py:139
  13.6 3.5 %collective-permute-start.2 = (f32[4,24,128]{2,1,0:T(8,128)S(1)}, f32[4,24,128]{2,1,0:T(8,128)S(1)}, u32[]{:S(2)}, u32[]{:S(2)}) collective-permute-start(f32[4,24,128]{2,1,0:T(8,128)S(1)} %get-tuple-element.38), channel_id=1, source_target_pairs={{0,1},{1,2},{2,3},{4,5},{5,6},{6,7},{8,9},{9,10},{10,11},{12,13},{... | collective-permute-start | bytes 147464 | tf_op jit(solution)/shard_map/ppermute | solution.py:139
  17.1 2.4 %collective-permute-start.3 = (f32[4,24,128]{2,1,0:T(8,128)S(1)}, f32[4,24,128]{2,1,0:T(8,128)S(1)}, u32[]{:S(2)}, u32[]{:S(2)}) collective-permute-start(f32[4,24,128]{2,1,0:T(8,128)S(1)} %get-tuple-element.33), channel_id=1, source_target_pairs={{1,0},{2,1},{3,2},{5,4},{6,5},{7,6},{9,8},{10,9},{11,10},{13,12},{... | collective-permute-start | bytes 147464 | tf_op jit(solution)/shard_map/ppermute | solution.py:139
  19.5 3.4 %shard_map.62 = (bf16[2,68,16,128]{3,2,1,0:T(8,128)(2,1)S(1)}, bf16[2,68,16,128]{3,2,1,0:T(8,128)(2,1)S(1)}, bf16[2,68,16,128]{3,2,1,0:T(8,128)(2,1)S(1)}) custom-call(s32[4]{0:T(128)S(1)} %pad_add_fusion.place_ref, bf16[2,64,16,512]{3,2,1,0:T(8,128)(2,1)S(1)} %copy-done.2), custom_call_target="tpu_custom_call" | custom-call | tf_op jit(solution)/shard_map/pallas_call | solution.py:28
  23.5 1.4 %collective-permute-start.4 = (bf16[2,68,16,128]{3,2,1,0:T(8,128)(2,1)S(1)}, bf16[2,68,16,128]{3,2,1,0:T(8,128)(2,1)S(1)}, u32[]{:S(2)}, u32[]{:S(2)}) collective-permute-start(bf16[2,68,16,128]{3,2,1,0:T(8,128)(2,1)S(1)} %get-tuple-element.42), channel_id=1, source_target_pairs={{0,1},{1,2},{2,3},{3,0},{4,5},{5,6},{6,7},{7,4},{8,9},{9,10},{10,1... | collective-permute-start | bytes 1671176 | tf_op jit(solution)/shard_map/ppermute | solution.py:368
  24.9 1.2 collective-permute-start.6
  26.1 7.6 %shard_map.63.grad_ref = f32[64,16,128]{2,1,0:T(8,128)S(1)} custom-call(s32[4]{0:T(128)S(1)} %pad_add_fusion.place_ref, f32[64]{0:T(128)S(1)} %copy-done.3, f32[64]{0:T(128)S(1)} %copy-done.4, f32[64,16,128]{2,1,0:T(8,128)S(1)} %copy-done, f32[4,24,128]{2,1,0:T(8,128)S(1)} %collective-permute-done.2.left_ref, ...), custom_call_target="tpu_custom_call" | custom-call | tf_op jit(solution)/shard_map/pallas_call | solution.py:28
  33.7 23.6 %collective-permute-done.5.refs_2_ = bf16[2,68,16,128]{3,2,1,0:T(8,128)(2,1)S(1)} collective-permute-done((bf16[2,68,16,128]{3,2,1,0:T(8,128)(2,1)S(1)}, bf16[2,68,16,128]{3,2,1,0:T(8,128)(2,1)S(1)}, u32[]{:S(2)}, u32[]{:S(2)}) %collective-permute-start.5) | collective-permute-done | bytes 557088 | tf_op jit(solution)/shard_map/ppermute | solution.py:368
  57.3 13.7 %collective-permute-done.4.refs_1_ = bf16[2,68,16,128]{3,2,1,0:T(8,128)(2,1)S(1)} collective-permute-done((bf16[2,68,16,128]{3,2,1,0:T(8,128)(2,1)S(1)}, bf16[2,68,16,128]{3,2,1,0:T(8,128)(2,1)S(1)}, u32[]{:S(2)}, u32[]{:S(2)}) %collective-permute-start.4) | collective-permute-done | bytes 557088 | tf_op jit(solution)/shard_map/ppermute | solution.py:368
  71.1 1.2 shard_map.64
  72.3 2.2 %collective-permute-start.8 = (bf16[8,16,128]{2,1,0:T(8,128)(2,1)S(1)}, bf16[8,16,128]{2,1,0:T(8,128)(2,1)S(1)}, u32[]{:S(2)}, u32[]{:S(2)}) collective-permute-start(bf16[8,16,128]{2,1,0:T(8,128)(2,1)S(1)} %get-tuple-element.45), channel_id=1, source_target_pairs={{1,0},{2,1},{3,2},{5,4},{6,5},{7,6},{9,8},{10,9},{11,10},{13,12},{... | collective-permute-start | bytes 98312 | tf_op jit(solution)/shard_map/ppermute | solution.py:139
  74.5 3.6 %collective-permute-start.7 = (bf16[8,16,128]{2,1,0:T(8,128)(2,1)S(1)}, bf16[8,16,128]{2,1,0:T(8,128)(2,1)S(1)}, u32[]{:S(2)}, u32[]{:S(2)}) collective-permute-start(bf16[8,16,128]{2,1,0:T(8,128)(2,1)S(1)} %get-tuple-element.45), channel_id=1, source_target_pairs={{0,1},{1,2},{2,3},{4,5},{5,6},{6,7},{8,9},{9,10},{10,11},{12,13},{... | collective-permute-start | bytes 98312 | tf_op jit(solution)/shard_map/ppermute | solution.py:139
  78.1 2.2 %collective-permute-done.7.left_ref = bf16[8,16,128]{2,1,0:T(8,128)(2,1)S(1)} collective-permute-done((bf16[8,16,128]{2,1,0:T(8,128)(2,1)S(1)}, bf16[8,16,128]{2,1,0:T(8,128)(2,1)S(1)}, u32[]{:S(2)}, u32[]{:S(2)}) %collective-permute-start.7) | collective-permute-done | bytes 32800 | tf_op jit(solution)/shard_map/ppermute | solution.py:139
  80.7 1.9 %collective-permute-start.10 = (bf16[16,16,128]{2,1,0:T(8,128)(2,1)S(1)}, bf16[16,16,128]{2,1,0:T(8,128)(2,1)S(1)}, u32[]{:S(2)}, u32[]{:S(2)}) collective-permute-start(bf16[16,16,128]{2,1,0:T(8,128)(2,1)S(1)} %get-tuple-element.47), channel_id=1, source_target_pairs={{4,0},{8,4},{12,8},{16,12},{20,16},{24,20},{28,24},{5,1},{9,5},{13... | collective-permute-start | bytes 196616 | tf_op jit(solution)/shard_map/ppermute | solution.py:139
  82.7 2.4 %collective-permute-start.9 = (bf16[16,16,128]{2,1,0:T(8,128)(2,1)S(1)}, bf16[16,16,128]{2,1,0:T(8,128)(2,1)S(1)}, u32[]{:S(2)}, u32[]{:S(2)}) collective-permute-start(bf16[16,16,128]{2,1,0:T(8,128)(2,1)S(1)} %get-tuple-element.47), channel_id=1, source_target_pairs={{0,4},{4,8},{8,12},{12,16},{16,20},{20,24},{24,28},{1,5},{5,9},{9,... | collective-permute-start | bytes 196616 | tf_op jit(solution)/shard_map/ppermute | solution.py:139
  85.1 4.1 %collective-permute-done.9.above_ref = bf16[16,16,128]{2,1,0:T(8,128)(2,1)S(1)} collective-permute-done((bf16[16,16,128]{2,1,0:T(8,128)(2,1)S(1)}, bf16[16,16,128]{2,1,0:T(8,128)(2,1)S(1)}, u32[]{:S(2)}, u32[]{:S(2)}) %collective-permute-start.9) | collective-permute-done | bytes 65568 | tf_op jit(solution)/shard_map/ppermute | solution.py:139
  89.1 1.5 %shard_map.66 = (f32[64,16,128]{2,1,0:T(8,128)S(1)}, f32[64,16,128]{2,1,0:T(8,128)S(1)}, f32[4,16,128]{2,1,0:T(8,128)S(1)}, f32[34,8,128]{2,1,0:T(8,128)S(1)}, f32[34,8,128]{2,1,0:T(8,128)S(1)}) custom-call(s32[4]{0:T(128)S(1)} %pad_add_fusion.place_ref, f32[64,16,128]{2,1,0:T(8,128)S(1)} %copy-done, f32[4,24,128]{2,1,0:T(8,128)S(1)} %collective-permute-done.2.left_ref, ...), custom_call_target="tpu_custom_call" | custom-call | tf_op jit(solution)/shard_map/pallas_call | solution.py:28
  90.7 1.9 %collective-permute-start.11 = (f32[34,8,128]{2,1,0:T(8,128)S(1)}, f32[34,8,128]{2,1,0:T(8,128)S(1)}, u32[]{:S(2)}, u32[]{:S(2)}) collective-permute-start(f32[34,8,128]{2,1,0:T(8,128)S(1)} %get-tuple-element.52), channel_id=1, source_target_pairs={{0,4},{4,8},{8,12},{12,16},{16,20},{20,24},{24,28},{1,5},{5,9},{9,... | collective-permute-start | bytes 417800 | tf_op jit(solution)/shard_map/ppermute | solution.py:139
  92.6 4.5 %collective-permute-start.12 = (f32[34,8,128]{2,1,0:T(8,128)S(1)}, f32[34,8,128]{2,1,0:T(8,128)S(1)}, u32[]{:S(2)}, u32[]{:S(2)}) collective-permute-start(f32[34,8,128]{2,1,0:T(8,128)S(1)} %get-tuple-element.53), channel_id=1, source_target_pairs={{4,0},{8,4},{12,8},{16,12},{20,16},{24,20},{28,24},{5,1},{9,5},{13... | collective-permute-start | bytes 417800 | tf_op jit(solution)/shard_map/ppermute | solution.py:139
  98.2 1.5 %collective-permute-done.12.below_ref = f32[34,8,128]{2,1,0:T(8,128)S(1)} collective-permute-done((f32[34,8,128]{2,1,0:T(8,128)S(1)}, f32[34,8,128]{2,1,0:T(8,128)S(1)}, u32[]{:S(2)}, u32[]{:S(2)}) %collective-permute-start.12) | collective-permute-done | bytes 139296 | tf_op jit(solution)/shard_map/ppermute | solution.py:139
  99.7 8.2 %shard_map.67 = (f32[8,16,128]{2,1,0:T(8,128)S(1)}, bf16[8,16,128]{2,1,0:T(8,128)(2,1)S(1)}) custom-call(s32[4]{0:T(128)S(1)} %pad_add_fusion.place_ref, f32[64]{0:T(128)S(1)} %copy-done.3, f32[64]{0:T(128)S(1)} %copy-done.4, f32[64,16,128]{2,1,0:T(8,128)S(1)} %get-tuple-element.49.x_ref.residual_ref, f32[4,16,128]{2,1,0:T(8,128)S(1)} %get-tuple-element.51.beside_ref, ...), custom_call_target="tpu_custom_call" | custom-call | tf_op jit(solution)/shard_map/pallas_call | solution.py:28
  108.0 1.9 %collective-permute-start.14 = (bf16[8,16,128]{2,1,0:T(8,128)(2,1)S(1)}, bf16[8,16,128]{2,1,0:T(8,128)(2,1)S(1)}, u32[]{:S(2)}, u32[]{:S(2)}) collective-permute-start(bf16[8,16,128]{2,1,0:T(8,128)(2,1)S(1)} %get-tuple-element.54), channel_id=1, source_target_pairs={{1,0},{2,1},{3,2},{5,4},{6,5},{7,6},{9,8},{10,9},{11,10},{13,12},{... | collective-permute-start | bytes 98312 | tf_op jit(solution)/shard_map/ppermute | solution.py:139
  109.9 3.9 %collective-permute-start.13 = (bf16[8,16,128]{2,1,0:T(8,128)(2,1)S(1)}, bf16[8,16,128]{2,1,0:T(8,128)(2,1)S(1)}, u32[]{:S(2)}, u32[]{:S(2)}) collective-permute-start(bf16[8,16,128]{2,1,0:T(8,128)(2,1)S(1)} %get-tuple-element.54), channel_id=1, source_target_pairs={{0,1},{1,2},{2,3},{4,5},{5,6},{6,7},{8,9},{9,10},{10,11},{12,13},{... | collective-permute-start | bytes 98312 | tf_op jit(solution)/shard_map/ppermute | solution.py:139
  113.8 1.9 %collective-permute-done.13.left_ref = bf16[8,16,128]{2,1,0:T(8,128)(2,1)S(1)} collective-permute-done((bf16[8,16,128]{2,1,0:T(8,128)(2,1)S(1)}, bf16[8,16,128]{2,1,0:T(8,128)(2,1)S(1)}, u32[]{:S(2)}, u32[]{:S(2)}) %collective-permute-start.13) | collective-permute-done | bytes 32800 | tf_op jit(solution)/shard_map/ppermute | solution.py:139
  116.0 3.5 %collective-permute-start.16 = (bf16[8,16,128]{2,1,0:T(8,128)(2,1)S(1)}, bf16[8,16,128]{2,1,0:T(8,128)(2,1)S(1)}, u32[]{:S(2)}, u32[]{:S(2)}) collective-permute-start(bf16[8,16,128]{2,1,0:T(8,128)(2,1)S(1)} %get-tuple-element.56), channel_id=1, source_target_pairs={{4,0},{8,4},{12,8},{16,12},{20,16},{24,20},{28,24},{5,1},{9,5},{13... | collective-permute-start | bytes 98312 | tf_op jit(solution)/shard_map/ppermute | solution.py:139
  119.5 1.9 %collective-permute-start.15 = (bf16[8,16,128]{2,1,0:T(8,128)(2,1)S(1)}, bf16[8,16,128]{2,1,0:T(8,128)(2,1)S(1)}, u32[]{:S(2)}, u32[]{:S(2)}) collective-permute-start(bf16[8,16,128]{2,1,0:T(8,128)(2,1)S(1)} %get-tuple-element.56), channel_id=1, source_target_pairs={{0,4},{4,8},{8,12},{12,16},{16,20},{20,24},{24,28},{1,5},{5,9},{9,... | collective-permute-start | bytes 98312 | tf_op jit(solution)/shard_map/ppermute | solution.py:139
  121.5 4.2 %collective-permute-done.15.above_ref = bf16[8,16,128]{2,1,0:T(8,128)(2,1)S(1)} collective-permute-done((bf16[8,16,128]{2,1,0:T(8,128)(2,1)S(1)}, bf16[8,16,128]{2,1,0:T(8,128)(2,1)S(1)}, u32[]{:S(2)}, u32[]{:S(2)}) %collective-permute-start.15) | collective-permute-done | bytes 32800 | tf_op jit(solution)/shard_map/ppermute | solution.py:139
  125.6 2.4 %shard_map.69 = (f32[64,16,128]{2,1,0:T(8,128)}, f32[64,16,128]{2,1,0:T(8,128)}) custom-call(s32[4]{0:T(128)S(1)} %pad_add_fusion.place_ref, f32[64,16,128]{2,1,0:T(8,128)S(1)} %get-tuple-element.49.x_ref.residual_ref, f32[64,16,128]{2,1,0:T(8,128)S(1)} %get-tuple-element.50.before_ref, bf16[8,16,128]{2,1,0:T(8,128)(2,1)S(1)} %collective-permute-done.15.above_ref, ...), custom_call_target="tpu_custom_call" | custom-call | tf_op jit(solution)/shard_map/pallas_call | solution.py:28
  (24 shorter events, 3.9 us)
Async XLA Ops:
  0.6 3.2 %copy-start = (f32[64,16,128]{2,1,0:T(8,128)S(1)}, f32[64,16,128]{2,1,0:T(8,128)}, u32[]{:S(2)}) copy-start(f32[64,16,128]{2,1,0:T(8,128)} %residual_ref) | copy-start | bytes 1572868
  0.7 1.6 %copy-start.1 = (bf16[2,64,16,512]{3,2,1,0:T(8,128)(2,1)S(1)}, bf16[2,64,16,512]{3,2,1,0:T(8,128)(2,1)}, u32[]{:S(2)}) copy-start(bf16[2,64,16,512]{3,2,1,0:T(8,128)(2,1)} %in_ref.2) | copy-start | bytes 6291460
  2.4 17.2 %copy-start.2 = (bf16[2,64,16,512]{3,2,1,0:T(8,128)(2,1)S(1)}, bf16[2,64,16,512]{3,2,1,0:T(8,128)(2,1)}, u32[]{:S(2)}) copy-start(bf16[2,64,16,512]{3,2,1,0:T(8,128)(2,1)} %in_ref.2) | copy-start | bytes 6291460
  3.9 22.2 %copy-start.3 = (f32[64]{0:T(128)S(1)}, f32[64]{0:T(128)}, u32[]{:S(2)}) copy-start(f32[64]{0:T(128)} %wx_ref.3) | copy-start | bytes 772
  3.9 22.2 %copy-start.4 = (f32[64]{0:T(128)S(1)}, f32[64]{0:T(128)}, u32[]{:S(2)}) copy-start(f32[64]{0:T(128)} %wy_ref.3) | copy-start | bytes 772
  3.9 7.2 %collective-permute-start = (f32[32,8,128]{2,1,0:T(8,128)S(1)}, f32[32,8,128]{2,1,0:T(8,128)S(1)}, u32[]{:S(2)}, u32[]{:S(2)}) collective-permute-start(f32[32,8,128]{2,1,0:T(8,128)S(1)} %get-tuple-element.31), channel_id=1, source_target_pairs={{0,4},{4,8},{8,12},{12,16},{16,20},{20,24},{24,28},{1,5},{5,9},{9,... | collective-permute-start | bytes 393224 | tf_op jit(solution)/shard_map/ppermute | solution.py:139
  5.9 7.0 %collective-permute-start.1 = (f32[32,8,128]{2,1,0:T(8,128)S(1)}, f32[32,8,128]{2,1,0:T(8,128)S(1)}, u32[]{:S(2)}, u32[]{:S(2)}) collective-permute-start(f32[32,8,128]{2,1,0:T(8,128)S(1)} %get-tuple-element.32), channel_id=1, source_target_pairs={{4,0},{8,4},{12,8},{16,12},{20,16},{24,20},{28,24},{5,1},{9,5},{13... | collective-permute-start | bytes 393224 | tf_op jit(solution)/shard_map/ppermute | solution.py:139
  13.6 9.3 %collective-permute-start.2 = (f32[4,24,128]{2,1,0:T(8,128)S(1)}, f32[4,24,128]{2,1,0:T(8,128)S(1)}, u32[]{:S(2)}, u32[]{:S(2)}) collective-permute-start(f32[4,24,128]{2,1,0:T(8,128)S(1)} %get-tuple-element.38), channel_id=1, source_target_pairs={{0,1},{1,2},{2,3},{4,5},{5,6},{6,7},{8,9},{9,10},{10,11},{12,13},{... | collective-permute-start | bytes 147464 | tf_op jit(solution)/shard_map/ppermute | solution.py:139
  17.1 6.4 %collective-permute-start.3 = (f32[4,24,128]{2,1,0:T(8,128)S(1)}, f32[4,24,128]{2,1,0:T(8,128)S(1)}, u32[]{:S(2)}, u32[]{:S(2)}) collective-permute-start(f32[4,24,128]{2,1,0:T(8,128)S(1)} %get-tuple-element.33), channel_id=1, source_target_pairs={{1,0},{2,1},{3,2},{5,4},{6,5},{7,6},{9,8},{10,9},{11,10},{13,12},{... | collective-permute-start | bytes 147464 | tf_op jit(solution)/shard_map/ppermute | solution.py:139
  19.5 37.9 %collective-permute-start.5 = (bf16[2,68,16,128]{3,2,1,0:T(8,128)(2,1)S(1)}, bf16[2,68,16,128]{3,2,1,0:T(8,128)(2,1)S(1)}, u32[]{:S(2)}, u32[]{:S(2)}) collective-permute-start(bf16[2,68,16,128]{3,2,1,0:T(8,128)(2,1)S(1)} %shard_map.59), channel_id=1, source_target_pairs={{0,2},{1,3},{2,0},{3,1},{4,6},{5,7},{6,4},{7,5},{8,10},{9,11},{10,... | collective-permute-start | bytes 1671176 | tf_op jit(solution)/shard_map/ppermute | solution.py:368
  23.5 47.6 %collective-permute-start.4 = (bf16[2,68,16,128]{3,2,1,0:T(8,128)(2,1)S(1)}, bf16[2,68,16,128]{3,2,1,0:T(8,128)(2,1)S(1)}, u32[]{:S(2)}, u32[]{:S(2)}) collective-permute-start(bf16[2,68,16,128]{3,2,1,0:T(8,128)(2,1)S(1)} %get-tuple-element.42), channel_id=1, source_target_pairs={{0,1},{1,2},{2,3},{3,0},{4,5},{5,6},{6,7},{7,4},{8,9},{9,10},{10,1... | collective-permute-start | bytes 1671176 | tf_op jit(solution)/shard_map/ppermute | solution.py:368
  24.9 46.2 %collective-permute-start.6 = (bf16[2,68,16,128]{3,2,1,0:T(8,128)(2,1)S(1)}, bf16[2,68,16,128]{3,2,1,0:T(8,128)(2,1)S(1)}, u32[]{:S(2)}, u32[]{:S(2)}) collective-permute-start(bf16[2,68,16,128]{3,2,1,0:T(8,128)(2,1)S(1)} %get-tuple-element.44), channel_id=1, source_target_pairs={{0,3},{1,0},{2,1},{3,2},{4,7},{5,4},{6,5},{7,6},{8,11},{9,8},{10,9... | collective-permute-start | bytes 1671176 | tf_op jit(solution)/shard_map/ppermute | solution.py:368
  72.3 5.9 %collective-permute-start.8 = (bf16[8,16,128]{2,1,0:T(8,128)(2,1)S(1)}, bf16[8,16,128]{2,1,0:T(8,128)(2,1)S(1)}, u32[]{:S(2)}, u32[]{:S(2)}) collective-permute-start(bf16[8,16,128]{2,1,0:T(8,128)(2,1)S(1)} %get-tuple-element.45), channel_id=1, source_target_pairs={{1,0},{2,1},{3,2},{5,4},{6,5},{7,6},{9,8},{10,9},{11,10},{13,12},{... | collective-permute-start | bytes 98312 | tf_op jit(solution)/shard_map/ppermute | solution.py:139
  74.5 5.8 %collective-permute-start.7 = (bf16[8,16,128]{2,1,0:T(8,128)(2,1)S(1)}, bf16[8,16,128]{2,1,0:T(8,128)(2,1)S(1)}, u32[]{:S(2)}, u32[]{:S(2)}) collective-permute-start(bf16[8,16,128]{2,1,0:T(8,128)(2,1)S(1)} %get-tuple-element.45), channel_id=1, source_target_pairs={{0,1},{1,2},{2,3},{4,5},{5,6},{6,7},{8,9},{9,10},{10,11},{12,13},{... | collective-permute-start | bytes 98312 | tf_op jit(solution)/shard_map/ppermute | solution.py:139
  80.7 4.3 %collective-permute-start.10 = (bf16[16,16,128]{2,1,0:T(8,128)(2,1)S(1)}, bf16[16,16,128]{2,1,0:T(8,128)(2,1)S(1)}, u32[]{:S(2)}, u32[]{:S(2)}) collective-permute-start(bf16[16,16,128]{2,1,0:T(8,128)(2,1)S(1)} %get-tuple-element.47), channel_id=1, source_target_pairs={{4,0},{8,4},{12,8},{16,12},{20,16},{24,20},{28,24},{5,1},{9,5},{13... | collective-permute-start | bytes 196616 | tf_op jit(solution)/shard_map/ppermute | solution.py:139
  82.7 6.5 %collective-permute-start.9 = (bf16[16,16,128]{2,1,0:T(8,128)(2,1)S(1)}, bf16[16,16,128]{2,1,0:T(8,128)(2,1)S(1)}, u32[]{:S(2)}, u32[]{:S(2)}) collective-permute-start(bf16[16,16,128]{2,1,0:T(8,128)(2,1)S(1)} %get-tuple-element.47), channel_id=1, source_target_pairs={{0,4},{4,8},{8,12},{12,16},{16,20},{20,24},{24,28},{1,5},{5,9},{9,... | collective-permute-start | bytes 196616 | tf_op jit(solution)/shard_map/ppermute | solution.py:139
  90.7 7.5 %collective-permute-start.11 = (f32[34,8,128]{2,1,0:T(8,128)S(1)}, f32[34,8,128]{2,1,0:T(8,128)S(1)}, u32[]{:S(2)}, u32[]{:S(2)}) collective-permute-start(f32[34,8,128]{2,1,0:T(8,128)S(1)} %get-tuple-element.52), channel_id=1, source_target_pairs={{0,4},{4,8},{8,12},{12,16},{16,20},{20,24},{24,28},{1,5},{5,9},{9,... | collective-permute-start | bytes 417800 | tf_op jit(solution)/shard_map/ppermute | solution.py:139
  92.6 7.1 %collective-permute-start.12 = (f32[34,8,128]{2,1,0:T(8,128)S(1)}, f32[34,8,128]{2,1,0:T(8,128)S(1)}, u32[]{:S(2)}, u32[]{:S(2)}) collective-permute-start(f32[34,8,128]{2,1,0:T(8,128)S(1)} %get-tuple-element.53), channel_id=1, source_target_pairs={{4,0},{8,4},{12,8},{16,12},{20,16},{24,20},{28,24},{5,1},{9,5},{13... | collective-permute-start | bytes 417800 | tf_op jit(solution)/shard_map/ppermute | solution.py:139
  108.0 5.9 %collective-permute-start.14 = (bf16[8,16,128]{2,1,0:T(8,128)(2,1)S(1)}, bf16[8,16,128]{2,1,0:T(8,128)(2,1)S(1)}, u32[]{:S(2)}, u32[]{:S(2)}) collective-permute-start(bf16[8,16,128]{2,1,0:T(8,128)(2,1)S(1)} %get-tuple-element.54), channel_id=1, source_target_pairs={{1,0},{2,1},{3,2},{5,4},{6,5},{7,6},{9,8},{10,9},{11,10},{13,12},{... | collective-permute-start | bytes 98312 | tf_op jit(solution)/shard_map/ppermute | solution.py:139
  109.9 5.8 %collective-permute-start.13 = (bf16[8,16,128]{2,1,0:T(8,128)(2,1)S(1)}, bf16[8,16,128]{2,1,0:T(8,128)(2,1)S(1)}, u32[]{:S(2)}, u32[]{:S(2)}) collective-permute-start(bf16[8,16,128]{2,1,0:T(8,128)(2,1)S(1)} %get-tuple-element.54), channel_id=1, source_target_pairs={{0,1},{1,2},{2,3},{4,5},{5,6},{6,7},{8,9},{9,10},{10,11},{12,13},{... | collective-permute-start | bytes 98312 | tf_op jit(solution)/shard_map/ppermute | solution.py:139
  116.0 5.5 %collective-permute-start.16 = (bf16[8,16,128]{2,1,0:T(8,128)(2,1)S(1)}, bf16[8,16,128]{2,1,0:T(8,128)(2,1)S(1)}, u32[]{:S(2)}, u32[]{:S(2)}) collective-permute-start(bf16[8,16,128]{2,1,0:T(8,128)(2,1)S(1)} %get-tuple-element.56), channel_id=1, source_target_pairs={{4,0},{8,4},{12,8},{16,12},{20,16},{24,20},{28,24},{5,1},{9,5},{13... | collective-permute-start | bytes 98312 | tf_op jit(solution)/shard_map/ppermute | solution.py:139
  119.5 6.1 %collective-permute-start.15 = (bf16[8,16,128]{2,1,0:T(8,128)(2,1)S(1)}, bf16[8,16,128]{2,1,0:T(8,128)(2,1)S(1)}, u32[]{:S(2)}, u32[]{:S(2)}) collective-permute-start(bf16[8,16,128]{2,1,0:T(8,128)(2,1)S(1)} %get-tuple-element.56), channel_id=1, source_target_pairs={{0,4},{4,8},{8,12},{12,16},{16,20},{20,24},{24,28},{1,5},{5,9},{9,... | collective-permute-start | bytes 98312 | tf_op jit(solution)/shard_map/ppermute | solution.py:139
where the time goes:
time: 129 us; the launch traced here: 128 us
  waiting for transfers between devices  55.4 us (43%)
  starting transfers between devices  42.9 us (33%)
  Pallas kernels  27.1 us (21%)
  local copies, waits for them, and re-layouts  1.66 us (1%)
    ppermute x14, starting transfers between devices, shift(): return lax.ppermute(x, axis, pairs)  40.2 us
    ppermute x3, waiting for transfers between devices, turned(): lax.ppermute(x, 'member', [(i, (i + step) % parts) for i in range(parts)])  37.4 us
    pallas_call x11, Pallas kernels, call(): pl.pallas_call(body, out_shape=out_shape, in_specs=in_specs or [VMEM] * l...  27.1 us
    ppermute x14, waiting for transfers between devices, shift(): return lax.ppermute(x, axis, pairs)  18 us
    ppermute x3, starting transfers between devices, turned(): lax.ppermute(x, 'member', [(i, (i + step) % parts) for i in range(parts)])  2.63 us
  transfers between devices with their start and end apart: 17, of which 11 were waited for; matrix products, arithmetic and copies ran while one was open for 0% of the time, Pallas kernels for 9%

commit v1 on v0

v1 whole, which is shorter than its diff:
```python
import functools

import jax
import jax.numpy as jnp
from jax import lax
from jax.experimental import pallas as pl
from jax.experimental.pallas import tpu as pltpu
from jax.sharding import PartitionSpec as P

ITERS = 2
MODEL_STEPS = 4
DIFFUSION = 0.1
RELAX = 0.5
REACH = 16
TAPER_TOTAL = sum(1.0 - (k / 17.0) ** 2 for k in range(-REACH, REACH + 1))
F32 = jnp.float32
BF16 = jnp.bfloat16
LANES = 128
SUB = 8
GROUP = LANES // (2 * MODEL_STEPS)

VMEM = pl.BlockSpec(memory_space=pltpu.VMEM)
SMEM = pl.BlockSpec(memory_space=pltpu.SMEM)
PARAMS = pltpu.CompilerParams(vmem_limit_bytes=48 * 1024 * 1024)


def call(body, out_shape, *args, in_specs=None, scratch=()):
    return pl.pallas_call(
        body,
        out_shape=out_shape,
        in_specs=in_specs or [VMEM] * len(args),
        out_specs=jax.tree.map(lambda _: VMEM, out_shape),
        scratch_shapes=scratch,
        compiler_params=PARAMS,
    )(*args)


def lane_iota(shape):
    return lax.broadcasted_iota(jnp.int32, shape, len(shape) - 1)


def sub_iota(shape):
    return lax.broadcasted_iota(jnp.int32, shape, len(shape) - 2)


def neighbor_of(place_ref, step):
    member, parts = place_ref[2], place_ref[3]
    return lax.rem(member + parts + step, parts)


def columns_split_body(in_ref, out_ref):
    parts, own, levels, rows, cols = out_ref.shape
    for c in range(parts):
        out_ref[c] = in_ref[:, :, :, c * cols : (c + 1) * cols]


def split_columns(members, parts):
    own, levels, rows, ny = members.shape
    out = jax.ShapeDtypeStruct((parts, own, levels, rows, ny // parts), members.dtype)
    return call(columns_split_body, out, members)


def put_left(x, k, total):
    here = lane_iota(x.shape) // MODEL_STEPS == GROUP - 1 - k
    return jnp.where(here, pltpu.roll(x, (MODEL_STEPS * (GROUP - k)) % LANES, 1), total)


def put_right(x, k, total):
    here = lane_iota(x.shape) // MODEL_STEPS == 2 * GROUP - 1 - k
    return jnp.where(here, pltpu.roll(x, (MODEL_STEPS * (2 * GROUP - 1 - k)) % LANES, 1), total)


def sides_body(place_ref, in_ref, *out_refs):
    own, groups, rows, _ = out_refs[0].shape
    cols = in_ref.shape[-1] // len(out_refs)

    def block(step):
        return pl.ds(pl.multiple_of(neighbor_of(place_ref, step) * cols, cols), cols)

    for r, out_ref in enumerate(out_refs):
        before, after = block(r - 1), block(r + 1)
        for m in range(own):

            def step(g, carry):
                total = jnp.zeros((rows, LANES), F32)
                for k in range(GROUP):
                    total = put_left(in_ref[m, g * GROUP + k, :, before].astype(F32), k, total)
                    total = put_right(in_ref[m, g * GROUP + k, :, after].astype(F32), k, total)
                out_ref[m, g] = total.astype(out_ref.dtype)
                return carry

            lax.fori_loop(0, groups, step, 0)


def side_columns(place, members, parts):
    own, levels, rows, ny = members.shape
    out = jax.ShapeDtypeStruct((own, levels // GROUP, rows, LANES), members.dtype)
    return call(sides_body, (out,) * parts, place, members, in_specs=[SMEM, VMEM])


def third_tile(below, above, odd):
    upper = sub_iota((SUB, LANES)) < MODEL_STEPS
    if odd:
        return jnp.where(upper, pltpu.roll(below, MODEL_STEPS, 0), above)
    return jnp.where(upper, below, pltpu.roll(above, MODEL_STEPS, 0))


def pack_rows(ref, at, top_ref, bottom_ref):
    upper = sub_iota((SUB, LANES)) < MODEL_STEPS
    count, rows, _ = ref.shape
    for q in range(count // 2):
        top_ref[at + q] = jnp.where(upper, ref[2 * q, :SUB], pltpu.roll(ref[2 * q + 1, :SUB], MODEL_STEPS, 0))
        bottom_ref[at + q] = jnp.where(
            upper, pltpu.roll(ref[2 * q, rows - SUB :], MODEL_STEPS, 0), ref[2 * q + 1, rows - SUB :]
        )


def rows_body(x_ref, top_ref, bottom_ref):
    pack_rows(x_ref, 0, top_ref, bottom_ref)


def edge_rows(x):
    out = jax.ShapeDtypeStruct((x.shape[0] // 2, SUB, LANES), F32)
    return call(rows_body, (out, out), x)


def columns_edge_body(x_ref, above_ref, below_ref, first_ref, last_ref):
    levels, rows, cols = x_ref.shape

    def step(g, carry):
        first = jnp.zeros((rows + SUB, LANES), F32)
        last = jnp.zeros((rows + SUB, LANES), F32)
        for k in range(GROUP):
            level = g * GROUP + k
            pair = g * (GROUP // 2) + k // 2
            x = jnp.concatenate([x_ref[level], third_tile(below_ref[pair], above_ref[pair], k % 2)], axis=0)
            last = put_left(x, k, last)
            first = put_right(x, k, first)
        first_ref[g] = first
        last_ref[g] = last
        return carry

    lax.fori_loop(0, levels // GROUP, step, 0)


def edge_columns(x, above, below):
    levels, rows, cols = x.shape
    out = jax.ShapeDtypeStruct((levels // GROUP, rows + SUB, LANES), F32)
    return call(columns_edge_body, (out, out), x, above, below)


def shift(x, axis, step):
    count = lax.axis_size(axis)
    pairs = [(i, i + step) for i in range(count) if 0 <= i + step < count]
    return lax.ppermute(x, axis, pairs)


def sweep(place_ref, wx_ref, wy_ref, x_ref, above_ref, below_ref, side_row, grad_ref):
    levels, rows, cols = x_ref.shape
    tile, tiles, member, parts = (place_ref[i] for i in range(4))
    x_flat = x_ref.reshape(levels * rows, cols)
    grad_flat = grad_ref.reshape(levels * rows, cols)
    halo = MODEL_STEPS
    pairs = above_ref.shape[0]
    above_flat = above_ref.reshape(pairs * SUB, LANES)
    below_flat = below_ref.reshape(pairs * SUB, LANES)

    lane = lane_iota((SUB, LANES))
    on_right = lane < halo
    is_first = lane == 0
    is_last = lane == LANES - 1
    inside = (on_right & (member < parts - 1)) | ((lane >= LANES - halo) & (member > 0))
    side_mask = jnp.where(inside, 1.0, 0.0).astype(F32)
    has_above = jnp.where(tile > 0, 1.0, 0.0).astype(F32)
    has_below = jnp.where(tile < tiles - 1, 1.0, 0.0).astype(F32)

    def load(g, half, e):
        q = 2 * g + half
        if e < 0:
            center = above_flat[pl.ds(q * SUB * halo + e + halo, SUB, stride=halo), :]
        elif e < rows:
            center = x_flat[pl.ds(q * SUB * rows + e, SUB, stride=rows), :]
        else:
            center = below_flat[pl.ds(q * SUB * halo + e - rows, SUB, stride=halo), :]
        row = jnp.broadcast_to(side_row(g, e), (SUB, LANES))
        start = halo * SUB * half
        right = pltpu.roll(row, start + halo, 1, stride=halo, stride_axis=0)
        left = pltpu.roll(row, start + LANES // 2, 1, stride=halo, stride_axis=0)
        return center, jnp.where(on_right, right, left) * side_mask

    def advance(before, here, after, e, own, ahead_x, ahead_y):
        center, side = here
        fore_c, fore_s = pltpu.roll(center, LANES - 1, 1), pltpu.roll(side, LANES - 1, 1)
        back_c, back_s = pltpu.roll(center, 1, 1), pltpu.roll(side, 1, 1)
        result = []
        for i, mine, fore, back in (
            (0, center, jnp.where(is_last, fore_s, fore_c), jnp.where(is_first, back_s, back_c)),
            (1, side, jnp.where(is_last, fore_c, fore_s), jnp.where(is_first, back_c, back_s)),
        ):
            value = own * mine + ahead_x * after[i] + ahead_y * fore + DIFFUSION * (before[i] + back)
            if e < 0:
                value = value * has_above
            if e >= rows:
                value = value * has_below
            result.append(value * side_mask if i else value)
        return tuple(result)

    def group(g, carry):
        for half in range(2):
            at = pl.ds(pl.multiple_of((2 * g + half) * SUB, SUB), SUB)
            wx, wy = wx_ref[at, :], wy_ref[at, :]
            coefficients = (1.0 - 4.0 * DIFFUSION - wx - wy, DIFFUSION + wx, DIFFUSION + wy)
            fields = [{} for _ in range(halo + 1)]
            for front in range(-halo, rows + halo):
                fields[0][front] = load(g, half, front)
                for n in range(1, halo + 1):
                    e = front - n
                    if -halo + n <= e < rows + halo - n:
                        old = fields[n - 1]
                        fields[n][e] = advance(old[e - 1], old[e], old[e + 1], e, *coefficients)
                        if n == halo:
                            grad_flat[pl.ds((2 * g + half) * SUB * rows + e, SUB, stride=rows), :] = fields[n][e][0]
        return carry

    lax.fori_loop(0, levels // GROUP, group, 0)


def first_model_body(place_ref, wx_ref, wy_ref, x_ref, left_ref, right_ref, above_ref, below_ref, grad_ref):
    rows = x_ref.shape[1]

    def side_row(g, e):
        at = pl.ds(e if e >= 0 else rows + SUB + e, 1)
        return left_ref[g, at, :] + right_ref[g, at, :]

    sweep(place_ref, wx_ref, wy_ref, x_ref, above_ref, below_ref, side_row, grad_ref)


def second_model_body(
    place_ref, wx_ref, wy_ref, x_ref, beside_ref, above_ref, below_ref, members_ref, wide_ref, thin_ref, grad_ref
):
    levels, rows, cols = x_ref.shape

    def side_row(g, e):
        if 0 <= e < rows:
            return beside_ref[g, pl.ds(e, 1), :]
        ref, row = (above_ref, e + MODEL_STEPS) if e < 0 else (below_ref, e - rows)
        flat = ref.reshape(ref.shape[0] * SUB, LANES)
        return flat[pl.ds((levels + g) * MODEL_STEPS + row, 1), :]

    sweep(place_ref, wx_ref, wy_ref, x_ref, above_ref, below_ref, side_row, grad_ref)
    project_body(grad_ref, members_ref, wide_ref, thin_ref)


def project_body(grad_ref, members_ref, wide_ref, thin_ref):
    parts, own, levels, rows, cols = members_ref.shape
    count = parts * own

    def step(q, carry):
        carry = list(carry)
        for u in range(2):
            g = grad_ref[2 * q + u]
            for m in range(count):
                carry[m] = carry[m] + members_ref[m // own, m % own, 2 * q + u].astype(F32) * g
        return tuple(carry)

    total = lax.fori_loop(0, levels // 2, step, (jnp.zeros((rows, cols), F32),) * count)
    for m in range(count):
        wide_ref[m] = total[m]
        thin_ref[m] = total[m].astype(BF16)


def taper(offset):
    k = offset.astype(F32)
    w = (1.0 - (k / 17.0) * (k / 17.0)) * (1.0 / TAPER_TOTAL)
    return jnp.where(jnp.abs(offset) <= REACH, w, 0.0)


def halves(x):
    high = x.astype(BF16)
    return high, (x - high.astype(F32)).astype(BF16)


def sharp_dot(a, b):
    ah, al = halves(a)
    bh, bl = halves(b)
    dot = functools.partial(jnp.dot, preferred_element_type=F32)
    return dot(ah, bh) + dot(al, bh) + dot(ah, bl)


def columns_body(left_ref, mid_ref, right_ref, wide_ref, thin_ref):
    count, rows, cols = mid_ref.shape
    wide = jnp.concatenate(
        [r[...].astype(F32).reshape(count * rows, cols) for r in (left_ref, mid_ref, right_ref)], axis=1
    )
    shape = (3 * cols, wide_ref.shape[0] // count * cols)
    lane = lane_iota(shape)
    beside = lane % MODEL_STEPS + jnp.where(lane < cols + LANES // 2, -MODEL_STEPS, cols)
    target = jnp.where(lane < cols, lane, beside)
    out = sharp_dot(wide, taper(sub_iota(shape) - cols - target))
    for i in range(shape[1] // cols):
        part = out[:, i * cols : (i + 1) * cols].reshape(count, rows, cols)
        wide_ref[i * count : (i + 1) * count] = part
        thin_ref[i * count : (i + 1) * count] = part.astype(BF16)


def smooth_rows(above_ref, mid_ref, below_ref):
    count, rows, cols = mid_ref.shape
    tall = jnp.concatenate(
        [
            jnp.concatenate([above_ref[m].astype(F32), mid_ref[m], below_ref[m].astype(F32)], axis=0)
            for m in range(count)
        ],
        axis=1,
    )
    shape = (rows, 3 * rows)
    out = sharp_dot(taper(lane_iota(shape) - sub_iota(shape) - rows), tall)
    return [out[:, m * cols : (m + 1) * cols] for m in range(count)]


def increments(members_ref, local, emit):
    parts, own, levels, rows, cols = members_ref.shape

    def step(q, carry):
        for u in range(2):
            level = 2 * q + u
            total = members_ref[0, 0, level].astype(F32) * local[0]
            for m in range(1, parts * own):
                total = total + members_ref[m // own, m % own, level].astype(F32) * local[m]
            emit(level, total)
        return carry

    lax.fori_loop(0, levels // 2, step, 0)


def update_body(
    place_ref, members_ref, residual_ref, left_ref, right_ref, above_ref, mid_ref, below_ref, *refs
):
    *side_refs, analysis_ref, out_ref, beside_ref, top_ref, bottom_ref, local_ref = refs
    levels, rows, cols = residual_ref.shape
    parts, own = members_ref.shape[:2]
    count = parts * own
    local = smooth_rows(above_ref, mid_ref, below_ref)
    for m in range(count):
        local_ref[m] = local[count + m]

    def emit(level, value):
        analysis_ref[level] = value
        out_ref[level] = residual_ref[level] - RELAX * value

    increments(members_ref, local, emit)
    for g in range(levels // GROUP):
        total = jnp.zeros((rows, LANES), F32)
        for m in range(count):
            at = neighbor_of(place_ref, -(m // own)) * own + m % own
            total = total + side_refs[m // own][m % own, g].astype(F32) * local_ref[at]
        beside_ref[g] = left_ref[g, :rows] + right_ref[g, :rows] - RELAX * total
    pack_rows(out_ref, 0, top_ref, bottom_ref)
    pack_rows(beside_ref, levels // 2, top_ref, bottom_ref)


def final_body(members_ref, residual_ref, before_ref, above_ref, mid_ref, below_ref, analysis_ref, out_ref):
    local = smooth_rows(above_ref, mid_ref, below_ref)

    def emit(level, value):
        analysis_ref[level] = before_ref[level] + value
        out_ref[level] = residual_ref[level] - RELAX * value

    increments(members_ref, local, emit)


def per_device(residual_in, members, wind_x, wind_y):
    levels, rows, cols = residual_in.shape
    tiles = lax.axis_size("tile")
    parts = lax.axis_size("member")
    place = jnp.stack([lax.axis_index("tile"), jnp.int32(tiles), lax.axis_index("member"), jnp.int32(parts)])
    count = members.shape[0] * parts
    groups = levels // GROUP

    def shape(*dims, kind=F32):
        return jax.ShapeDtypeStruct(dims, kind)

    def both(*dims):
        return shape(*dims), shape(*dims, kind=BF16)

    def turned(x, step):
        return lax.ppermute(x, "member", [(i, (i + step) % parts) for i in range(parts)])

    def smoothed(wide, thin, planes):
        wide, thin = call(
            columns_body, both(planes, rows, cols), shift(thin, "member", 1), wide, shift(thin, "member", -1)
        )
        return shift(thin, "tile", 1), wide, shift(thin, "tile", -1)

    like = shape(levels, rows, cols)
    halo = shape((levels + groups) // 2, SUB, LANES)
    wind_x, wind_y = (jnp.broadcast_to(w[:, None], (levels, LANES)) for w in (wind_x, wind_y))

    soon, residual_in = lax.optimization_barrier((split_columns(members, parts), residual_in))
    block = lax.all_to_all(soon, "member", split_axis=0, concat_axis=0, tiled=True)
    top, bottom = edge_rows(residual_in)
    above, below = shift(bottom, "tile", 1), shift(top, "tile", -1)
    first, last = edge_columns(residual_in, above, below)
    left, right = shift(last, "member", 1), shift(first, "member", -1)
    members, first = lax.optimization_barrier((members, first))
    sides, left, right = lax.optimization_barrier((side_columns(place, members, parts), left, right))
    sides = [turned(x, r) if r else x for r, x in enumerate(sides)]
    grad = call(
        first_model_body, like,
        place, wind_x, wind_y, residual_in, left, right, above, below, in_specs=[SMEM] + [VMEM] * 7,
    )
    grad, sides = lax.optimization_barrier((grad, sides))
    wide, thin = call(project_body, both(count, rows, cols), grad, block)

    analysis, residual, beside, top, bottom = call(
        update_body, (like, like, shape(groups, rows, LANES), halo, halo),
        place, block, residual_in, left, right, *smoothed(wide, thin, 2 * count), *sides,
        in_specs=[SMEM] + [VMEM] * (7 + parts), scratch=[pltpu.VMEM((count, rows, cols), F32)],
    )
    above, below = shift(bottom, "tile", 1), shift(top, "tile", -1)
    wide, thin = call(
        second_model_body, both(count, rows, cols),
        place, wind_x, wind_y, residual, beside, above, below, block,
        in_specs=[SMEM] + [VMEM] * 7, scratch=[pltpu.VMEM((levels, rows, cols), F32)],
    )
    return call(final_body, (like, like), block, residual, analysis, *smoothed(wide, thin, count))


def solution(mesh):
    return jax.shard_map(
        per_device,
        mesh=mesh,
        in_specs=(P(None, "tile", "member"), P("member", None, "tile", None), P(), P()),
        out_specs=(P(None, "tile", "member"), P(None, "tile", "member")),
        check_vma=False,
    )
```

time: 129 us -> 129 us (level)
  waiting for transfers between devices: 55.4 us -> 45.7 us
  starting transfers between devices: 42.9 us -> 48.9 us
  local copies, waits for them, and re-layouts: 1.66 us -> 6.55 us
    ppermute x3, waiting for transfers between devices: 37.4 us -> 0.01 us  [turned(): lax.ppermute(x, 'member', [(i, (i + step) % parts) for i in range(parts)])]
    ppermute x14, waiting for transfers between devices: 18 us -> 45.7 us  [shift(): return lax.ppermute(x, axis, pairs)]
    all_to_all x0 -> x1, starting transfers between devices: none -> 5.34 us  [per_device(): lax.all_to_all(soon, 'member', split_axis=0, concat_axis=0, tiled=True)]
    unnamed x10 -> x32, local copies, waits for them, and re-layouts: 1.66 us -> 6.41 us
  transfers between devices with their start and end apart: 17 -> 18, of which waited for: 11 -> 9; matrix products, arithmetic and copies ran while one was open for 0% -> 0% of each run, Pallas kernels for 9% -> 10%
where the time goes in v1:
time: 129 us; the launch traced here: 128 us
  starting transfers between devices  48.9 us (38%)
  waiting for transfers between devices  45.7 us (35%)
  Pallas kernels  26.1 us (20%)
  local copies, waits for them, and re-layouts  6.55 us (5%)
    ppermute x14, waiting for transfers between devices, shift(): return lax.ppermute(x, axis, pairs)  45.7 us
    ppermute x14, starting transfers between devices, shift(): return lax.ppermute(x, axis, pairs)  40 us
    pallas_call x11, Pallas kernels, call(): pl.pallas_call(body, out_shape=out_shape, in_specs=in_specs or [VMEM] * l...  26.1 us
    unnamed x32, local copies, waits for them, and re-layouts  6.41 us
    all_to_all x1, starting transfers between devices, per_device(): lax.all_to_all(soon, 'member', split_axis=0, concat_axis=0, tiled=True)  5.34 us
    ppermute x3, starting transfers between devices, turned(): lax.ppermute(x, 'member', [(i, (i + step) % parts) for i in range(parts)])  3.63 us
  transfers between devices with their start and end apart: 18, of which 9 were waited for; matrix products, arithmetic and copies ran while one was open for 0% of the time, Pallas kernels for 10%

profile of v1, /device:TPU:20, one launch (start us, length us, event | category | flops | bytes accessed | tf_op | source)
XLA Modules:
  0.0 128.3 jit_solution(9074128852156537328)
XLA Ops:
  0.6 1.6 %copy-done.1 = bf16[2,64,16,512]{3,2,1,0:T(8,128)(2,1)S(1)} copy-done((bf16[2,64,16,512]{3,2,1,0:T(8,128)(2,1)S(1)}, bf16[2,64,16,512]{3,2,1,0:T(8,128)(2,1)}, u32[]{:S(2)}) %copy-start.1) | copy-done | bytes 2097176
  2.6 1.4 %copy-done.3 = bf16[4,2,64,16,128]{4,3,2,1,0:T(8,128)(2,1)} copy-done((bf16[4,2,64,16,128]{4,3,2,1,0:T(8,128)(2,1)}, bf16[4,2,64,16,128]{4,3,2,1,0:T(8,128)(2,1)S(1)}, u32[]{:S(2)}) %copy-start.3) | copy-done | bytes 2097176
  4.0 5.3 %all-to-all-start = ((bf16[4,2,64,16,128]{4,3,2,1,0:T(8,128)(2,1)}), bf16[4,2,64,16,128]{4,3,2,1,0:T(8,128)(2,1)S(1)}, u32[]{:S(2)}, u32[]{:S(2)}) async-start(bf16[4,2,64,16,128]{4,3,2,1,0:T(8,128)(2,1)} %copy-done.3), calls=%async_computation | async-start | bytes 4194304 | tf_op jit(solution)/shard_map/all_to_all | solution.py:399
  9.3 1.9 %collective-permute-start = (f32[32,8,128]{2,1,0:T(8,128)S(1)}, f32[32,8,128]{2,1,0:T(8,128)S(1)}, u32[]{:S(2)}, u32[]{:S(2)}) collective-permute-start(f32[32,8,128]{2,1,0:T(8,128)S(1)} %get-tuple-element.39), channel_id=1, source_target_pairs={{0,4},{4,8},{8,12},{12,16},{16,20},{20,24},{24,28},{1,5},{5,9},{9,... | collective-permute-start | bytes 393224 | tf_op jit(solution)/shard_map/ppermute | solution.py:155
  11.3 4.5 %collective-permute-start.1 = (f32[32,8,128]{2,1,0:T(8,128)S(1)}, f32[32,8,128]{2,1,0:T(8,128)S(1)}, u32[]{:S(2)}, u32[]{:S(2)}) collective-permute-start(f32[32,8,128]{2,1,0:T(8,128)S(1)} %get-tuple-element.40), channel_id=1, source_target_pairs={{4,0},{8,4},{12,8},{16,12},{20,16},{24,20},{28,24},{5,1},{9,5},{13... | collective-permute-start | bytes 393224 | tf_op jit(solution)/shard_map/ppermute | solution.py:155
  16.5 1.8 %collective-permute-done.1.below_ref = f32[32,8,128]{2,1,0:T(8,128)S(1)} collective-permute-done((f32[32,8,128]{2,1,0:T(8,128)S(1)}, f32[32,8,128]{2,1,0:T(8,128)S(1)}, u32[]{:S(2)}, u32[]{:S(2)}) %collective-permute-start.1) | collective-permute-done | bytes 131104 | tf_op jit(solution)/shard_map/ppermute | solution.py:155
  19.0 3.4 %collective-permute-start.2 = (f32[4,24,128]{2,1,0:T(8,128)S(1)}, f32[4,24,128]{2,1,0:T(8,128)S(1)}, u32[]{:S(2)}, u32[]{:S(2)}) collective-permute-start(f32[4,24,128]{2,1,0:T(8,128)S(1)} %get-tuple-element.47), channel_id=1, source_target_pairs={{0,1},{1,2},{2,3},{4,5},{5,6},{6,7},{8,9},{9,10},{10,11},{12,13},{... | collective-permute-start | bytes 147464 | tf_op jit(solution)/shard_map/ppermute | solution.py:155
  22.4 2.5 %collective-permute-start.3 = (f32[4,24,128]{2,1,0:T(8,128)S(1)}, f32[4,24,128]{2,1,0:T(8,128)S(1)}, u32[]{:S(2)}, u32[]{:S(2)}) collective-permute-start(f32[4,24,128]{2,1,0:T(8,128)S(1)} %get-tuple-element.41), channel_id=1, source_target_pairs={{1,0},{2,1},{3,2},{5,4},{6,5},{7,6},{9,8},{10,9},{11,10},{13,12},{... | collective-permute-start | bytes 147464 | tf_op jit(solution)/shard_map/ppermute | solution.py:155
  24.9 1.6 %copy-done.2 = bf16[2,64,16,512]{3,2,1,0:T(8,128)(2,1)S(1)} copy-done((bf16[2,64,16,512]{3,2,1,0:T(8,128)(2,1)S(1)}, bf16[2,64,16,512]{3,2,1,0:T(8,128)(2,1)}, u32[]{:S(2)}) %copy-start.2) | copy-done | bytes 2097176
  26.5 4.0 %shard_map.62 = (bf16[2,4,16,128]{3,2,1,0:T(8,128)(2,1)S(1)}, bf16[2,4,16,128]{3,2,1,0:T(8,128)(2,1)S(1)}, bf16[2,4,16,128]{3,2,1,0:T(8,128)(2,1)S(1)}, bf16[2,4,16,128]{3,2,1,0:T(8,128)(2,1)S(1)}) custom-call(s32[4]{0:T(128)S(1)} %pad_add_fusion.place_ref, bf16[2,64,16,512]{3,2,1,0:T(8,128)(2,1)S(1)} %copy-done.2), custom_call_target="tpu_custom_call" | custom-call | tf_op jit(solution)/shard_map/pallas_call | solution.py:28
  30.5 25.7 %collective-permute-done.2.left_ref = f32[4,24,128]{2,1,0:T(8,128)S(1)} collective-permute-done((f32[4,24,128]{2,1,0:T(8,128)S(1)}, f32[4,24,128]{2,1,0:T(8,128)S(1)}, u32[]{:S(2)}, u32[]{:S(2)}) %collective-permute-start.2) | collective-permute-done | bytes 49184 | tf_op jit(solution)/shard_map/ppermute | solution.py:155
  56.2 3.6 %collective-permute-start.5 = (bf16[2,4,16,128]{3,2,1,0:T(8,128)(2,1)S(1)}, bf16[2,4,16,128]{3,2,1,0:T(8,128)(2,1)S(1)}, u32[]{:S(2)}, u32[]{:S(2)}) collective-permute-start(bf16[2,4,16,128]{3,2,1,0:T(8,128)(2,1)S(1)} %get-tuple-element.52), channel_id=1, source_target_pairs={{0,2},{1,3},{2,0},{3,1},{4,6},{5,7},{6,4},{7,5},{8,10},{9,11},{10,... | collective-permute-start | bytes 98312 | tf_op jit(solution)/shard_map/ppermute | solution.py:386
  60.0 8.0 %shard_map.63.grad_ref = f32[64,16,128]{2,1,0:T(8,128)S(1)} custom-call(s32[4]{0:T(128)S(1)} %pad_add_fusion.place_ref, f32[64,128]{1,0:T(8,128)S(1)} %broadcast_in_dim.4.wx_ref, f32[64,128]{1,0:T(8,128)S(1)} %broadcast_in_dim.5.wy_ref, f32[64,16,128]{2,1,0:T(8,128)S(1)} %copy-done, f32[4,24,128]{2,1,0:T(8,128)S(1)} %collective-permute-done.2.left_ref, ...), custom_call_target="tpu_custom_call" | custom-call | tf_op jit(solution)/shard_map/pallas_call | solution.py:28
  70.5 2.5 %collective-permute-start.8 = (bf16[8,16,128]{2,1,0:T(8,128)(2,1)S(1)}, bf16[8,16,128]{2,1,0:T(8,128)(2,1)S(1)}, u32[]{:S(2)}, u32[]{:S(2)}) collective-permute-start(bf16[8,16,128]{2,1,0:T(8,128)(2,1)S(1)} %get-tuple-element.55), channel_id=1, source_target_pairs={{1,0},{2,1},{3,2},{5,4},{6,5},{7,6},{9,8},{10,9},{11,10},{13,12},{... | collective-permute-start | bytes 98312 | tf_op jit(solution)/shard_map/ppermute | solution.py:155
  72.9 3.4 %collective-permute-start.7 = (bf16[8,16,128]{2,1,0:T(8,128)(2,1)S(1)}, bf16[8,16,128]{2,1,0:T(8,128)(2,1)S(1)}, u32[]{:S(2)}, u32[]{:S(2)}) collective-permute-start(bf16[8,16,128]{2,1,0:T(8,128)(2,1)S(1)} %get-tuple-element.55), channel_id=1, source_target_pairs={{0,1},{1,2},{2,3},{4,5},{5,6},{6,7},{8,9},{9,10},{10,11},{12,13},{... | collective-permute-start | bytes 98312 | tf_op jit(solution)/shard_map/ppermute | solution.py:155
  76.3 2.8 %collective-permute-done.7.left_ref = bf16[8,16,128]{2,1,0:T(8,128)(2,1)S(1)} collective-permute-done((bf16[8,16,128]{2,1,0:T(8,128)(2,1)S(1)}, bf16[8,16,128]{2,1,0:T(8,128)(2,1)S(1)}, u32[]{:S(2)}, u32[]{:S(2)}) %collective-permute-start.7) | collective-permute-done | bytes 32800 | tf_op jit(solution)/shard_map/ppermute | solution.py:155
  79.5 1.9 %collective-permute-start.10 = (bf16[16,16,128]{2,1,0:T(8,128)(2,1)S(1)}, bf16[16,16,128]{2,1,0:T(8,128)(2,1)S(1)}, u32[]{:S(2)}, u32[]{:S(2)}) collective-permute-start(bf16[16,16,128]{2,1,0:T(8,128)(2,1)S(1)} %get-tuple-element.57), channel_id=1, source_target_pairs={{4,0},{8,4},{12,8},{16,12},{20,16},{24,20},{28,24},{5,1},{9,5},{13... | collective-permute-start | bytes 196616 | tf_op jit(solution)/shard_map/ppermute | solution.py:155
  81.4 2.4 %collective-permute-start.9 = (bf16[16,16,128]{2,1,0:T(8,128)(2,1)S(1)}, bf16[16,16,128]{2,1,0:T(8,128)(2,1)S(1)}, u32[]{:S(2)}, u32[]{:S(2)}) collective-permute-start(bf16[16,16,128]{2,1,0:T(8,128)(2,1)S(1)} %get-tuple-element.57), channel_id=1, source_target_pairs={{0,4},{4,8},{8,12},{12,16},{16,20},{20,24},{24,28},{1,5},{5,9},{9,... | collective-permute-start | bytes 196616 | tf_op jit(solution)/shard_map/ppermute | solution.py:155
  83.8 4.1 %collective-permute-done.9.above_ref = bf16[16,16,128]{2,1,0:T(8,128)(2,1)S(1)} collective-permute-done((bf16[16,16,128]{2,1,0:T(8,128)(2,1)S(1)}, bf16[16,16,128]{2,1,0:T(8,128)(2,1)S(1)}, u32[]{:S(2)}, u32[]{:S(2)}) %collective-permute-start.9) | collective-permute-done | bytes 65568 | tf_op jit(solution)/shard_map/ppermute | solution.py:155
  87.9 1.5 %shard_map.66 = (f32[64,16,128]{2,1,0:T(8,128)S(1)}, f32[64,16,128]{2,1,0:T(8,128)S(1)}, f32[4,16,128]{2,1,0:T(8,128)S(1)}, f32[34,8,128]{2,1,0:T(8,128)S(1)}, f32[34,8,128]{2,1,0:T(8,128)S(1)}) custom-call(s32[4]{0:T(128)S(1)} %copy-done.13, bf16[4,2,64,16,128]{4,3,2,1,0:T(8,128)(2,1)S(1)} %all-to-all-done.members_ref, f32[64,16,128]{2,1,0:T(8,128)S(1)} %copy-done, ...), custom_call_target="tpu_custom_call" | custom-call | tf_op jit(solution)/shard_map/pallas_call | solution.py:28
  89.4 1.9 %collective-permute-start.11 = (f32[34,8,128]{2,1,0:T(8,128)S(1)}, f32[34,8,128]{2,1,0:T(8,128)S(1)}, u32[]{:S(2)}, u32[]{:S(2)}) collective-permute-start(f32[34,8,128]{2,1,0:T(8,128)S(1)} %get-tuple-element.66), channel_id=1, source_target_pairs={{0,4},{4,8},{8,12},{12,16},{16,20},{20,24},{24,28},{1,5},{5,9},{9,... | collective-permute-start | bytes 417800 | tf_op jit(solution)/shard_map/ppermute | solution.py:155
  91.4 4.5 %collective-permute-start.12 = (f32[34,8,128]{2,1,0:T(8,128)S(1)}, f32[34,8,128]{2,1,0:T(8,128)S(1)}, u32[]{:S(2)}, u32[]{:S(2)}) collective-permute-start(f32[34,8,128]{2,1,0:T(8,128)S(1)} %get-tuple-element.67), channel_id=1, source_target_pairs={{4,0},{8,4},{12,8},{16,12},{20,16},{24,20},{28,24},{5,1},{9,5},{13... | collective-permute-start | bytes 417800 | tf_op jit(solution)/shard_map/ppermute | solution.py:155
  95.9 0.8 collective-permute-done.11.above_ref
  96.7 1.8 %collective-permute-done.12.below_ref = f32[34,8,128]{2,1,0:T(8,128)S(1)} collective-permute-done((f32[34,8,128]{2,1,0:T(8,128)S(1)}, f32[34,8,128]{2,1,0:T(8,128)S(1)}, u32[]{:S(2)}, u32[]{:S(2)}) %collective-permute-start.12) | collective-permute-done | bytes 139296 | tf_op jit(solution)/shard_map/ppermute | solution.py:155
  98.5 8.5 %shard_map.67 = (f32[8,16,128]{2,1,0:T(8,128)S(1)}, bf16[8,16,128]{2,1,0:T(8,128)(2,1)S(1)}) custom-call(s32[4]{0:T(128)S(1)} %copy-done.13, f32[64,128]{1,0:T(8,128)S(1)} %broadcast_in_dim.4.wx_ref, f32[64,128]{1,0:T(8,128)S(1)} %broadcast_in_dim.5.wy_ref, f32[64,16,128]{2,1,0:T(8,128)S(1)} %get-tuple-element.63.x_ref.residual_ref, ...), custom_call_target="tpu_custom_call" | custom-call | tf_op jit(solution)/shard_map/pallas_call | solution.py:28
  107.0 3.9 %collective-permute-start.14 = (bf16[8,16,128]{2,1,0:T(8,128)(2,1)S(1)}, bf16[8,16,128]{2,1,0:T(8,128)(2,1)S(1)}, u32[]{:S(2)}, u32[]{:S(2)}) collective-permute-start(bf16[8,16,128]{2,1,0:T(8,128)(2,1)S(1)} %get-tuple-element.68), channel_id=1, source_target_pairs={{1,0},{2,1},{3,2},{5,4},{6,5},{7,6},{9,8},{10,9},{11,10},{13,12},{... | collective-permute-start | bytes 98312 | tf_op jit(solution)/shard_map/ppermute | solution.py:155
  111.0 1.9 %collective-permute-start.13 = (bf16[8,16,128]{2,1,0:T(8,128)(2,1)S(1)}, bf16[8,16,128]{2,1,0:T(8,128)(2,1)S(1)}, u32[]{:S(2)}, u32[]{:S(2)}) collective-permute-start(bf16[8,16,128]{2,1,0:T(8,128)(2,1)S(1)} %get-tuple-element.68), channel_id=1, source_target_pairs={{0,1},{1,2},{2,3},{4,5},{5,6},{6,7},{8,9},{9,10},{10,11},{12,13},{... | collective-permute-start | bytes 98312 | tf_op jit(solution)/shard_map/ppermute | solution.py:155
  112.9 3.9 %collective-permute-done.13.left_ref = bf16[8,16,128]{2,1,0:T(8,128)(2,1)S(1)} collective-permute-done((bf16[8,16,128]{2,1,0:T(8,128)(2,1)S(1)}, bf16[8,16,128]{2,1,0:T(8,128)(2,1)S(1)}, u32[]{:S(2)}, u32[]{:S(2)}) %collective-permute-start.13) | collective-permute-done | bytes 32800 | tf_op jit(solution)/shard_map/ppermute | solution.py:155
  117.0 3.3 %collective-permute-start.16 = (bf16[8,16,128]{2,1,0:T(8,128)(2,1)S(1)}, bf16[8,16,128]{2,1,0:T(8,128)(2,1)S(1)}, u32[]{:S(2)}, u32[]{:S(2)}) collective-permute-start(bf16[8,16,128]{2,1,0:T(8,128)(2,1)S(1)} %get-tuple-element.70), channel_id=1, source_target_pairs={{4,0},{8,4},{12,8},{16,12},{20,16},{24,20},{28,24},{5,1},{9,5},{13... | collective-permute-start | bytes 98312 | tf_op jit(solution)/shard_map/ppermute | solution.py:155
  120.3 1.9 %collective-permute-start.15 = (bf16[8,16,128]{2,1,0:T(8,128)(2,1)S(1)}, bf16[8,16,128]{2,1,0:T(8,128)(2,1)S(1)}, u32[]{:S(2)}, u32[]{:S(2)}) collective-permute-start(bf16[8,16,128]{2,1,0:T(8,128)(2,1)S(1)} %get-tuple-element.70), channel_id=1, source_target_pairs={{0,4},{4,8},{8,12},{12,16},{16,20},{20,24},{24,28},{1,5},{5,9},{9,... | collective-permute-start | bytes 98312 | tf_op jit(solution)/shard_map/ppermute | solution.py:155
  122.3 4.2 %collective-permute-done.15.above_ref = bf16[8,16,128]{2,1,0:T(8,128)(2,1)S(1)} collective-permute-done((bf16[8,16,128]{2,1,0:T(8,128)(2,1)S(1)}, bf16[8,16,128]{2,1,0:T(8,128)(2,1)S(1)}, u32[]{:S(2)}, u32[]{:S(2)}) %collective-permute-start.15) | collective-permute-done | bytes 32800 | tf_op jit(solution)/shard_map/ppermute | solution.py:155
  126.4 1.8 %shard_map.69 = (f32[64,16,128]{2,1,0:T(8,128)}, f32[64,16,128]{2,1,0:T(8,128)}) custom-call(bf16[4,2,64,16,128]{4,3,2,1,0:T(8,128)(2,1)S(1)} %all-to-all-done.members_ref, f32[64,16,128]{2,1,0:T(8,128)S(1)} %get-tuple-element.63.x_ref.residual_ref, f32[64,16,128]{2,1,0:T(8,128)S(1)} %get-tuple-element.64.before_ref, ...), custom_call_target="tpu_custom_call" | custom-call | tf_op jit(solution)/shard_map/pallas_call | solution.py:28
  (50 shorter events, 5.1 us)
Async XLA Ops:
  0.6 1.6 %copy-start.1 = (bf16[2,64,16,512]{3,2,1,0:T(8,128)(2,1)S(1)}, bf16[2,64,16,512]{3,2,1,0:T(8,128)(2,1)}, u32[]{:S(2)}) copy-start(bf16[2,64,16,512]{3,2,1,0:T(8,128)(2,1)} %in_ref.2) | copy-start | bytes 6291460
  2.6 1.4 %copy-start.3 = (bf16[4,2,64,16,128]{4,3,2,1,0:T(8,128)(2,1)}, bf16[4,2,64,16,128]{4,3,2,1,0:T(8,128)(2,1)S(1)}, u32[]{:S(2)}) copy-start(bf16[4,2,64,16,128]{4,3,2,1,0:T(8,128)(2,1)S(1)} %shard_map.59) | copy-start | bytes 6291460
  4.0 5.3 %copy-start = (f32[64,16,128]{2,1,0:T(8,128)S(1)}, f32[64,16,128]{2,1,0:T(8,128)}, u32[]{:S(2)}) copy-start(f32[64,16,128]{2,1,0:T(8,128)} %residual_ref) | copy-start | bytes 1572868
  4.0 65.9 %all-to-all-start = ((bf16[4,2,64,16,128]{4,3,2,1,0:T(8,128)(2,1)}), bf16[4,2,64,16,128]{4,3,2,1,0:T(8,128)(2,1)S(1)}, u32[]{:S(2)}, u32[]{:S(2)}) async-start(bf16[4,2,64,16,128]{4,3,2,1,0:T(8,128)(2,1)} %copy-done.3), calls=%async_computation | async-start | bytes 4194304 | tf_op jit(solution)/shard_map/all_to_all | solution.py:399
  9.3 50.5 %copy-start.14 = (f32[64]{0:T(128)S(1)}, f32[64]{0:T(128)}, u32[]{:S(2)}) copy-start(f32[64]{0:T(128)} %param.6) | copy-start | bytes 772
  9.3 50.6 %copy-start.15 = (f32[64]{0:T(128)S(1)}, f32[64]{0:T(128)}, u32[]{:S(2)}) copy-start(f32[64]{0:T(128)} %param.7) | copy-start | bytes 772
  9.3 7.2 %collective-permute-start = (f32[32,8,128]{2,1,0:T(8,128)S(1)}, f32[32,8,128]{2,1,0:T(8,128)S(1)}, u32[]{:S(2)}, u32[]{:S(2)}) collective-permute-start(f32[32,8,128]{2,1,0:T(8,128)S(1)} %get-tuple-element.39), channel_id=1, source_target_pairs={{0,4},{4,8},{8,12},{12,16},{16,20},{20,24},{24,28},{1,5},{5,9},{9,... | collective-permute-start | bytes 393224 | tf_op jit(solution)/shard_map/ppermute | solution.py:155
  11.3 7.0 %collective-permute-start.1 = (f32[32,8,128]{2,1,0:T(8,128)S(1)}, f32[32,8,128]{2,1,0:T(8,128)S(1)}, u32[]{:S(2)}, u32[]{:S(2)}) collective-permute-start(f32[32,8,128]{2,1,0:T(8,128)S(1)} %get-tuple-element.40), channel_id=1, source_target_pairs={{4,0},{8,4},{12,8},{16,12},{20,16},{24,20},{28,24},{5,1},{9,5},{13... | collective-permute-start | bytes 393224 | tf_op jit(solution)/shard_map/ppermute | solution.py:155
  19.0 37.2 %collective-permute-start.2 = (f32[4,24,128]{2,1,0:T(8,128)S(1)}, f32[4,24,128]{2,1,0:T(8,128)S(1)}, u32[]{:S(2)}, u32[]{:S(2)}) collective-permute-start(f32[4,24,128]{2,1,0:T(8,128)S(1)} %get-tuple-element.47), channel_id=1, source_target_pairs={{0,1},{1,2},{2,3},{4,5},{5,6},{6,7},{8,9},{9,10},{10,11},{12,13},{... | collective-permute-start | bytes 147464 | tf_op jit(solution)/shard_map/ppermute | solution.py:155
  22.4 33.8 %collective-permute-start.3 = (f32[4,24,128]{2,1,0:T(8,128)S(1)}, f32[4,24,128]{2,1,0:T(8,128)S(1)}, u32[]{:S(2)}, u32[]{:S(2)}) collective-permute-start(f32[4,24,128]{2,1,0:T(8,128)S(1)} %get-tuple-element.41), channel_id=1, source_target_pairs={{1,0},{2,1},{3,2},{5,4},{6,5},{7,6},{9,8},{10,9},{11,10},{13,12},{... | collective-permute-start | bytes 147464 | tf_op jit(solution)/shard_map/ppermute | solution.py:155
  24.9 1.6 %copy-start.2 = (bf16[2,64,16,512]{3,2,1,0:T(8,128)(2,1)S(1)}, bf16[2,64,16,512]{3,2,1,0:T(8,128)(2,1)}, u32[]{:S(2)}) copy-start(bf16[2,64,16,512]{3,2,1,0:T(8,128)(2,1)} %in_ref.2) | copy-start | bytes 6291460
  26.5 42.1 %copy-start.12 = (s32[4]{0:T(128)}, s32[4]{0:T(128)S(1)}, u32[]{:S(2)}) copy-start(s32[4]{0:T(128)S(1)} %pad_add_fusion.place_ref) | copy-start | bytes 52
  56.2 12.4 %copy-start.4 = (f32[4,24,128]{2,1,0:T(8,128)}, f32[4,24,128]{2,1,0:T(8,128)S(1)}, u32[]{:S(2)}) copy-start(f32[4,24,128]{2,1,0:T(8,128)S(1)} %collective-permute-done.3.right_ref) | copy-start | bytes 147460
  56.2 11.8 %collective-permute-start.4 = (bf16[2,4,16,128]{3,2,1,0:T(8,128)(2,1)S(1)}, bf16[2,4,16,128]{3,2,1,0:T(8,128)(2,1)S(1)}, u32[]{:S(2)}, u32[]{:S(2)}) collective-permute-start(bf16[2,4,16,128]{3,2,1,0:T(8,128)(2,1)S(1)} %get-tuple-element.51), channel_id=1, source_target_pairs={{0,1},{1,2},{2,3},{3,0},{4,5},{5,6},{6,7},{7,4},{8,9},{9,10},{10,1... | collective-permute-start | bytes 98312 | tf_op jit(solution)/shard_map/ppermute | solution.py:386
  56.2 12.4 %collective-permute-start.5 = (bf16[2,4,16,128]{3,2,1,0:T(8,128)(2,1)S(1)}, bf16[2,4,16,128]{3,2,1,0:T(8,128)(2,1)S(1)}, u32[]{:S(2)}, u32[]{:S(2)}) collective-permute-start(bf16[2,4,16,128]{3,2,1,0:T(8,128)(2,1)S(1)} %get-tuple-element.52), channel_id=1, source_target_pairs={{0,2},{1,3},{2,0},{3,1},{4,6},{5,7},{6,4},{7,5},{8,10},{9,11},{10,... | collective-permute-start | bytes 98312 | tf_op jit(solution)/shard_map/ppermute | solution.py:386
  59.8 9.4 %collective-permute-start.6 = (bf16[2,4,16,128]{3,2,1,0:T(8,128)(2,1)S(1)}, bf16[2,4,16,128]{3,2,1,0:T(8,128)(2,1)S(1)}, u32[]{:S(2)}, u32[]{:S(2)}) collective-permute-start(bf16[2,4,16,128]{3,2,1,0:T(8,128)(2,1)S(1)} %get-tuple-element.53), channel_id=1, source_target_pairs={{0,3},{1,0},{2,1},{3,2},{4,7},{5,4},{6,5},{7,6},{8,11},{9,8},{10,9... | collective-permute-start | bytes 98312 | tf_op jit(solution)/shard_map/ppermute | solution.py:386
  68.6 0.6 copy-start.8
  69.2 18.7 %copy-start.7 = (bf16[2,4,16,128]{3,2,1,0:T(8,128)(2,1)S(1)}, bf16[2,4,16,128]{3,2,1,0:T(8,128)(2,1)}, u32[]{:S(2)}) copy-start(bf16[2,4,16,128]{3,2,1,0:T(8,128)(2,1)} %copy-done.6) | copy-start | bytes 98308
  69.9 18.0 %copy-start.5 = (f32[4,24,128]{2,1,0:T(8,128)S(1)}, f32[4,24,128]{2,1,0:T(8,128)}, u32[]{:S(2)}) copy-start(f32[4,24,128]{2,1,0:T(8,128)} %copy-done.4) | copy-start | bytes 147460
  69.9 18.0 %copy-start.9 = (bf16[2,4,16,128]{3,2,1,0:T(8,128)(2,1)S(1)}, bf16[2,4,16,128]{3,2,1,0:T(8,128)(2,1)}, u32[]{:S(2)}) copy-start(bf16[2,4,16,128]{3,2,1,0:T(8,128)(2,1)} %copy-done.8) | copy-start | bytes 98308
  69.9 18.1 %copy-start.13 = (s32[4]{0:T(128)S(1)}, s32[4]{0:T(128)}, u32[]{:S(2)}) copy-start(s32[4]{0:T(128)} %copy-done.12) | copy-start | bytes 52
  69.9 18.1 %copy-start.11 = (bf16[2,4,16,128]{3,2,1,0:T(8,128)(2,1)S(1)}, bf16[2,4,16,128]{3,2,1,0:T(8,128)(2,1)}, u32[]{:S(2)}) copy-start(bf16[2,4,16,128]{3,2,1,0:T(8,128)(2,1)} %copy-done.10) | copy-start | bytes 98308
  70.5 5.9 %collective-permute-start.8 = (bf16[8,16,128]{2,1,0:T(8,128)(2,1)S(1)}, bf16[8,16,128]{2,1,0:T(8,128)(2,1)S(1)}, u32[]{:S(2)}, u32[]{:S(2)}) collective-permute-start(bf16[8,16,128]{2,1,0:T(8,128)(2,1)S(1)} %get-tuple-element.55), channel_id=1, source_target_pairs={{1,0},{2,1},{3,2},{5,4},{6,5},{7,6},{9,8},{10,9},{11,10},{13,12},{... | collective-permute-start | bytes 98312 | tf_op jit(solution)/shard_map/ppermute | solution.py:155
  72.9 6.2 %collective-permute-start.7 = (bf16[8,16,128]{2,1,0:T(8,128)(2,1)S(1)}, bf16[8,16,128]{2,1,0:T(8,128)(2,1)S(1)}, u32[]{:S(2)}, u32[]{:S(2)}) collective-permute-start(bf16[8,16,128]{2,1,0:T(8,128)(2,1)S(1)} %get-tuple-element.55), channel_id=1, source_target_pairs={{0,1},{1,2},{2,3},{4,5},{5,6},{6,7},{8,9},{9,10},{10,11},{12,13},{... | collective-permute-start | bytes 98312 | tf_op jit(solution)/shard_map/ppermute | solution.py:155
  79.5 4.3 %collective-permute-start.10 = (bf16[16,16,128]{2,1,0:T(8,128)(2,1)S(1)}, bf16[16,16,128]{2,1,0:T(8,128)(2,1)S(1)}, u32[]{:S(2)}, u32[]{:S(2)}) collective-permute-start(bf16[16,16,128]{2,1,0:T(8,128)(2,1)S(1)} %get-tuple-element.57), channel_id=1, source_target_pairs={{4,0},{8,4},{12,8},{16,12},{20,16},{24,20},{28,24},{5,1},{9,5},{13... | collective-permute-start | bytes 196616 | tf_op jit(solution)/shard_map/ppermute | solution.py:155
  81.4 6.5 %collective-permute-start.9 = (bf16[16,16,128]{2,1,0:T(8,128)(2,1)S(1)}, bf16[16,16,128]{2,1,0:T(8,128)(2,1)S(1)}, u32[]{:S(2)}, u32[]{:S(2)}) collective-permute-start(bf16[16,16,128]{2,1,0:T(8,128)(2,1)S(1)} %get-tuple-element.57), channel_id=1, source_target_pairs={{0,4},{4,8},{8,12},{12,16},{16,20},{20,24},{24,28},{1,5},{5,9},{9,... | collective-permute-start | bytes 196616 | tf_op jit(solution)/shard_map/ppermute | solution.py:155
  89.4 7.3 %collective-permute-start.11 = (f32[34,8,128]{2,1,0:T(8,128)S(1)}, f32[34,8,128]{2,1,0:T(8,128)S(1)}, u32[]{:S(2)}, u32[]{:S(2)}) collective-permute-start(f32[34,8,128]{2,1,0:T(8,128)S(1)} %get-tuple-element.66), channel_id=1, source_target_pairs={{0,4},{4,8},{8,12},{12,16},{16,20},{20,24},{24,28},{1,5},{5,9},{9,... | collective-permute-start | bytes 417800 | tf_op jit(solution)/shard_map/ppermute | solution.py:155
  91.4 7.1 %collective-permute-start.12 = (f32[34,8,128]{2,1,0:T(8,128)S(1)}, f32[34,8,128]{2,1,0:T(8,128)S(1)}, u32[]{:S(2)}, u32[]{:S(2)}) collective-permute-start(f32[34,8,128]{2,1,0:T(8,128)S(1)} %get-tuple-element.67), channel_id=1, source_target_pairs={{4,0},{8,4},{12,8},{16,12},{20,16},{24,20},{28,24},{5,1},{9,5},{13... | collective-permute-start | bytes 417800 | tf_op jit(solution)/shard_map/ppermute | solution.py:155
  107.0 5.9 %collective-permute-start.14 = (bf16[8,16,128]{2,1,0:T(8,128)(2,1)S(1)}, bf16[8,16,128]{2,1,0:T(8,128)(2,1)S(1)}, u32[]{:S(2)}, u32[]{:S(2)}) collective-permute-start(bf16[8,16,128]{2,1,0:T(8,128)(2,1)S(1)} %get-tuple-element.68), channel_id=1, source_target_pairs={{1,0},{2,1},{3,2},{5,4},{6,5},{7,6},{9,8},{10,9},{11,10},{13,12},{... | collective-permute-start | bytes 98312 | tf_op jit(solution)/shard_map/ppermute | solution.py:155
  111.0 5.8 %collective-permute-start.13 = (bf16[8,16,128]{2,1,0:T(8,128)(2,1)S(1)}, bf16[8,16,128]{2,1,0:T(8,128)(2,1)S(1)}, u32[]{:S(2)}, u32[]{:S(2)}) collective-permute-start(bf16[8,16,128]{2,1,0:T(8,128)(2,1)S(1)} %get-tuple-element.68), channel_id=1, source_target_pairs={{0,1},{1,2},{2,3},{4,5},{5,6},{6,7},{8,9},{9,10},{10,11},{12,13},{... | collective-permute-start | bytes 98312 | tf_op jit(solution)/shard_map/ppermute | solution.py:155
  117.0 5.2 %collective-permute-start.16 = (bf16[8,16,128]{2,1,0:T(8,128)(2,1)S(1)}, bf16[8,16,128]{2,1,0:T(8,128)(2,1)S(1)}, u32[]{:S(2)}, u32[]{:S(2)}) collective-permute-start(bf16[8,16,128]{2,1,0:T(8,128)(2,1)S(1)} %get-tuple-element.70), channel_id=1, source_target_pairs={{4,0},{8,4},{12,8},{16,12},{20,16},{24,20},{28,24},{5,1},{9,5},{13... | collective-permute-start | bytes 98312 | tf_op jit(solution)/shard_map/ppermute | solution.py:155
  120.3 6.1 %collective-permute-start.15 = (bf16[8,16,128]{2,1,0:T(8,128)(2,1)S(1)}, bf16[8,16,128]{2,1,0:T(8,128)(2,1)S(1)}, u32[]{:S(2)}, u32[]{:S(2)}) collective-permute-start(bf16[8,16,128]{2,1,0:T(8,128)(2,1)S(1)} %get-tuple-element.70), channel_id=1, source_target_pairs={{0,4},{4,8},{8,12},{12,16},{16,20},{20,24},{24,28},{1,5},{5,9},{9,... | collective-permute-start | bytes 98312 | tf_op jit(solution)/shard_map/ppermute | solution.py:155
  (2 other events, 1.2 us)

commit v2 on v1

v2 whole, which is shorter than its diff:
```python
import functools

import jax
import jax.numpy as jnp
from jax import lax
from jax.experimental import pallas as pl
from jax.experimental.pallas import tpu as pltpu
from jax.sharding import PartitionSpec as P

ITERS = 2
MODEL_STEPS = 4
DIFFUSION = 0.1
RELAX = 0.5
REACH = 16
TAPER_TOTAL = sum(1.0 - (k / 17.0) ** 2 for k in range(-REACH, REACH + 1))
F32 = jnp.float32
BF16 = jnp.bfloat16
LANES = 128
SUB = 8
GROUP = LANES // (2 * MODEL_STEPS)

VMEM = pl.BlockSpec(memory_space=pltpu.VMEM)
SMEM = pl.BlockSpec(memory_space=pltpu.SMEM)
PARAMS = pltpu.CompilerParams(vmem_limit_bytes=48 * 1024 * 1024)


def call(body, out_shape, *args, in_specs=None, scratch=()):
    return pl.pallas_call(
        body,
        out_shape=out_shape,
        in_specs=in_specs or [VMEM] * len(args),
        out_specs=jax.tree.map(lambda _: VMEM, out_shape),
        scratch_shapes=scratch,
        compiler_params=PARAMS,
    )(*args)


def lane_iota(shape):
    return lax.broadcasted_iota(jnp.int32, shape, len(shape) - 1)


def sub_iota(shape):
    return lax.broadcasted_iota(jnp.int32, shape, len(shape) - 2)


def neighbor_of(place_ref, step):
    member, parts = place_ref[2], place_ref[3]
    return lax.rem(member + parts + step, parts)


def columns_split_body(place_ref, in_ref, *out_refs):
    cols = out_refs[0].shape[-1]
    for r, out_ref in enumerate(out_refs):
        out_ref[...] = in_ref[:, :, :, pl.ds(pl.multiple_of(neighbor_of(place_ref, r) * cols, cols), cols)]


def split_columns(place, members, parts):
    own, levels, rows, ny = members.shape
    out = jax.ShapeDtypeStruct((own, levels, rows, ny // parts), members.dtype)
    return call(columns_split_body, (out,) * parts, place, members, in_specs=[SMEM, VMEM])


def left_slot(k):
    return 3 * SUB - 1 - k % SUB - GROUP * (k // SUB)


def put_left(x, k, total):
    here = lane_iota(x.shape) // MODEL_STEPS == left_slot(k)
    return jnp.where(here, pltpu.roll(x, (MODEL_STEPS * (left_slot(k) + 1)) % LANES, 1), total)


def put_right(x, k, total):
    here = lane_iota(x.shape) // MODEL_STEPS == left_slot(k) + SUB
    return jnp.where(here, pltpu.roll(x, MODEL_STEPS * (left_slot(k) + SUB), 1), total)


def sides_body(place_ref, in_ref, *out_refs):
    own, groups, rows, _ = out_refs[0].shape
    cols = in_ref.shape[-1] // len(out_refs)

    def block(step):
        return pl.ds(pl.multiple_of(neighbor_of(place_ref, step) * cols, cols), cols)

    for r, out_ref in enumerate(out_refs):
        before, after = block(r - 1), block(r + 1)
        for m in range(own):

            def step(g, carry):
                total = jnp.zeros((rows, LANES), F32)
                for k in range(GROUP):
                    total = put_left(in_ref[m, g * GROUP + k, :, before].astype(F32), k, total)
                    total = put_right(in_ref[m, g * GROUP + k, :, after].astype(F32), k, total)
                out_ref[m, g] = total.astype(out_ref.dtype)
                return carry

            lax.fori_loop(0, groups, step, 0)


def side_columns(place, members, parts):
    own, levels, rows, ny = members.shape
    out = jax.ShapeDtypeStruct((own, levels // GROUP, rows, LANES), members.dtype)
    return call(sides_body, (out,) * parts, place, members, in_specs=[SMEM, VMEM])


def pack_rows(ref, at, top_ref, bottom_ref):
    upper = sub_iota((SUB, LANES)) < MODEL_STEPS
    count, rows, _ = ref.shape
    for q in range(count // 2):
        top_ref[at + q] = jnp.where(upper, ref[2 * q, :SUB], pltpu.roll(ref[2 * q + 1, :SUB], MODEL_STEPS, 0))
        bottom_ref[at + q] = jnp.where(
            upper, pltpu.roll(ref[2 * q, rows - SUB :], MODEL_STEPS, 0), ref[2 * q + 1, rows - SUB :]
        )


def rows_body(x_ref, left_ref, right_ref, beside_ref, top_ref, bottom_ref):
    beside_ref[...] = left_ref[...] + right_ref[...]
    pack_rows(x_ref, 0, top_ref, bottom_ref)
    pack_rows(beside_ref, x_ref.shape[0] // 2, top_ref, bottom_ref)


def columns_edge_body(x_ref, first_ref, last_ref):
    levels, rows, cols = x_ref.shape
    for g in range(levels // GROUP):
        first = jnp.zeros((rows, LANES), F32)
        last = jnp.zeros((rows, LANES), F32)
        for k in range(GROUP):
            last = put_left(x_ref[g * GROUP + k], k, last)
            first = put_right(x_ref[g * GROUP + k], k, first)
        first_ref[g] = first
        last_ref[g] = last


def shift(x, axis, step):
    count = lax.axis_size(axis)
    pairs = [(i, i + step) for i in range(count) if 0 <= i + step < count]
    return lax.ppermute(x, axis, pairs)


def sweep(place_ref, wx_ref, wy_ref, x_ref, above_ref, below_ref, side_row, grad_ref):
    levels, rows, cols = x_ref.shape
    tile, tiles, member, parts = (place_ref[i] for i in range(4))
    x_flat = x_ref.reshape(levels * rows, cols)
    grad_flat = grad_ref.reshape(levels * rows, cols)
    halo = MODEL_STEPS
    pairs = above_ref.shape[0]
    above_flat = above_ref.reshape(pairs * SUB, LANES)
    below_flat = below_ref.reshape(pairs * SUB, LANES)

    half = LANES // 2
    lane = lane_iota((SUB, LANES))
    on_right = lane % half < halo
    first_of = (lane == 0, lane == half)
    last_of = (lane == LANES - 1, lane == half - 1)
    second = (lane >= half // 2) & (lane < half + half // 2)
    inside = (on_right & (member < parts - 1)) | ((lane % half >= half - halo) & (member > 0))
    side_mask = jnp.where(inside, 1.0, 0.0).astype(F32)
    has_above = jnp.where(tile > 0, 1.0, 0.0).astype(F32)
    has_below = jnp.where(tile < tiles - 1, 1.0, 0.0).astype(F32)

    def load(g, e):
        centers = []
        for q in (2 * g, 2 * g + 1):
            if e < 0:
                centers.append(above_flat[pl.ds(q * SUB * halo + e + halo, SUB, stride=halo), :])
            elif e < rows:
                centers.append(x_flat[pl.ds(q * SUB * rows + e, SUB, stride=rows), :])
            else:
                centers.append(below_flat[pl.ds(q * SUB * halo + e - rows, SUB, stride=halo), :])
        row = jnp.broadcast_to(side_row(g, e), (SUB, LANES))
        right = pltpu.roll(row, halo, 1, stride=halo, stride_axis=0)
        left = pltpu.roll(row, LANES // 4, 1, stride=halo, stride_axis=0)
        side = jnp.where(on_right, right, left) * side_mask
        return centers[0], pltpu.roll(centers[1], half, 1), side

    def advance(before, here, after, e, coefficients):
        fore = [pltpu.roll(x, LANES - 1, 1) for x in here]
        back = [pltpu.roll(x, 1, 1) for x in here]
        fore_side = jnp.where(last_of[0], fore[0], jnp.where(last_of[1], fore[1], fore[2]))
        back_side = jnp.where(first_of[0], back[0], jnp.where(first_of[1], back[1], back[2]))
        fores = [jnp.where(last_of[i], fore[2], fore[i]) for i in range(2)] + [fore_side]
        backs = [jnp.where(first_of[i], back[2], back[i]) for i in range(2)] + [back_side]
        result = []
        for i, (own, ahead_x, ahead_y) in enumerate(coefficients):
            value = own * here[i] + ahead_x * after[i] + ahead_y * fores[i] + DIFFUSION * (before[i] + backs[i])
            if e < 0:
                value = value * has_above
            if e >= rows:
                value = value * has_below
            result.append(value * side_mask if i == 2 else value)
        return tuple(result)

    def group(g, carry):
        coefficients = []
        for q in (2 * g, 2 * g + 1):
            at = pl.ds(pl.multiple_of(q * SUB, SUB), SUB)
            wx, wy = wx_ref[at, :], wy_ref[at, :]
            coefficients.append((1.0 - 4.0 * DIFFUSION - wx - wy, DIFFUSION + wx, DIFFUSION + wy))
        coefficients.append(tuple(jnp.where(second, b, a) for a, b in zip(*coefficients)))
        fields = [{} for _ in range(halo + 1)]
        for front in range(-halo, rows + halo):
            fields[0][front] = load(g, front)
            for n in range(1, halo + 1):
                e = front - n
                if -halo + n <= e < rows + halo - n:
                    old = fields[n - 1]
                    fields[n][e] = advance(old[e - 1], old[e], old[e + 1], e, coefficients)
            e = front - halo
            if 0 <= e < rows:
                grad_flat[pl.ds(2 * g * SUB * rows + e, SUB, stride=rows), :] = fields[halo][e][0]
                grad_flat[pl.ds((2 * g + 1) * SUB * rows + e, SUB, stride=rows), :] = pltpu.roll(fields[halo][e][1], half, 1)
        return carry

    lax.fori_loop(0, levels // GROUP, group, 0)


def side_rows(levels, rows, beside_ref, above_ref, below_ref):
    above_flat, below_flat = (ref.reshape(ref.shape[0] * SUB, LANES) for ref in (above_ref, below_ref))

    def side_row(g, e):
        if 0 <= e < rows:
            return beside_ref[g, pl.ds(e, 1), :]
        flat, row = (above_flat, e + MODEL_STEPS) if e < 0 else (below_flat, e - rows)
        return flat[pl.ds((levels + g) * MODEL_STEPS + row, 1), :]

    return side_row


def first_model_body(place_ref, wx_ref, wy_ref, x_ref, beside_ref, above_ref, below_ref, grad_ref):
    levels, rows, cols = x_ref.shape
    side_row = side_rows(levels, rows, beside_ref, above_ref, below_ref)
    sweep(place_ref, wx_ref, wy_ref, x_ref, above_ref, below_ref, side_row, grad_ref)


def second_model_body(place_ref, wx_ref, wy_ref, x_ref, beside_ref, above_thin_ref, below_thin_ref, *refs):
    *others, grad_ref, above_ref, below_ref = refs
    levels, rows, cols = x_ref.shape
    above_ref[...] = above_thin_ref[...].astype(F32).reshape(above_ref.shape)
    below_ref[...] = below_thin_ref[...].astype(F32).reshape(below_ref.shape)
    side_row = side_rows(levels, rows, beside_ref, above_ref, below_ref)
    sweep(place_ref, wx_ref, wy_ref, x_ref, above_ref, below_ref, side_row, grad_ref)
    project_body(place_ref, grad_ref, *others)


def project_body(place_ref, grad_ref, *refs):
    *member_refs, wide_ref, thin_ref = refs
    own, _, rows, cols = member_refs[0].shape
    count = len(member_refs) * own

    def step(q, carry):
        carry = list(carry)
        for u in range(2):
            g = grad_ref[2 * q + u]
            for m in range(count):
                carry[m] = carry[m] + member_refs[m // own][m % own, 2 * q + u].astype(F32) * g
        return tuple(carry)

    total = lax.fori_loop(0, grad_ref.shape[0] // 2, step, (jnp.zeros((rows, cols), F32),) * count)
    for m in range(count):
        at = neighbor_of(place_ref, -(m // own)) * own + m % own
        wide_ref[at] = total[m]
        thin_ref[at] = total[m].astype(BF16)


def taper(offset):
    k = offset.astype(F32)
    w = (1.0 - (k / 17.0) * (k / 17.0)) * (1.0 / TAPER_TOTAL)
    return jnp.where(jnp.abs(offset) <= REACH, w, 0.0)


def halves(x):
    high = x.astype(BF16)
    return high, (x - high.astype(F32)).astype(BF16)


def sharp_dot(a, b):
    ah, al = halves(a)
    bh, bl = halves(b)
    dot = functools.partial(jnp.dot, preferred_element_type=F32)
    return dot(ah, bh) + dot(al, bh) + dot(ah, bl)


def columns_body(left_ref, mid_ref, right_ref, wide_ref, thin_ref):
    count, rows, cols = mid_ref.shape
    wide = jnp.concatenate(
        [r[...].astype(F32).reshape(count * rows, cols) for r in (left_ref, mid_ref, right_ref)], axis=1
    )
    shape = (3 * cols, wide_ref.shape[0] // count * cols)
    lane = lane_iota(shape)
    beside = lane % MODEL_STEPS + jnp.where((lane // (SUB * MODEL_STEPS)) % 2 == 0, -MODEL_STEPS, cols)
    target = jnp.where(lane < cols, lane, beside)
    out = sharp_dot(wide, taper(sub_iota(shape) - cols - target))
    for i in range(shape[1] // cols):
        part = out[:, i * cols : (i + 1) * cols].reshape(count, rows, cols)
        wide_ref[i * count : (i + 1) * count] = part
        thin_ref[i * count : (i + 1) * count] = part.astype(BF16)


def smooth_rows(above_ref, mid_ref, below_ref):
    count, rows, cols = mid_ref.shape
    tall = jnp.concatenate(
        [
            jnp.concatenate([above_ref[m].astype(F32), mid_ref[m], below_ref[m].astype(F32)], axis=0)
            for m in range(count)
        ],
        axis=1,
    )
    shape = (rows, 3 * rows)
    out = sharp_dot(taper(lane_iota(shape) - sub_iota(shape) - rows), tall)
    return [out[:, m * cols : (m + 1) * cols] for m in range(count)]


def increments(place_ref, member_refs, local_ref, levels, emit):
    own = member_refs[0].shape[0]
    count = len(member_refs) * own
    local = [local_ref[neighbor_of(place_ref, -(m // own)) * own + m % own] for m in range(count)]

    def step(q, carry):
        for u in range(2):
            level = 2 * q + u
            total = member_refs[0][0, level].astype(F32) * local[0]
            for m in range(1, count):
                total = total + member_refs[m // own][m % own, level].astype(F32) * local[m]
            emit(level, total)
        return carry

    lax.fori_loop(0, levels // 2, step, 0)


def update_body(parts, place_ref, residual_ref, around_ref, above_ref, mid_ref, below_ref, *refs):
    member_refs, side_refs = refs[:parts], refs[parts : 2 * parts]
    analysis_ref, out_ref, beside_ref, top_ref, bottom_ref, local_ref, top_wide_ref, bottom_wide_ref = refs[2 * parts :]
    levels, rows, cols = residual_ref.shape
    own = member_refs[0].shape[0]
    count = parts * own
    for m, value in enumerate(smooth_rows(above_ref, mid_ref, below_ref)):
        local_ref[m] = value

    def emit(level, value):
        analysis_ref[level] = value
        out_ref[level] = residual_ref[level] - RELAX * value

    increments(place_ref, member_refs, local_ref, levels, emit)
    for g in range(levels // GROUP):
        total = jnp.zeros((rows, LANES), F32)
        for m in range(count):
            at = neighbor_of(place_ref, -(m // own)) * own + m % own
            total = total + side_refs[m // own][m % own, g].astype(F32) * local_ref[count + at]
        beside_ref[g] = around_ref[g] - RELAX * total
    pack_rows(out_ref, 0, top_wide_ref, bottom_wide_ref)
    pack_rows(beside_ref, levels // 2, top_wide_ref, bottom_wide_ref)
    top_ref[...] = top_wide_ref[...].reshape(top_ref.shape).astype(BF16)
    bottom_ref[...] = bottom_wide_ref[...].reshape(bottom_ref.shape).astype(BF16)


def final_body(parts, place_ref, residual_ref, before_ref, above_ref, mid_ref, below_ref, *refs):
    member_refs = refs[:parts]
    analysis_ref, out_ref, local_ref = refs[parts:]
    for m, value in enumerate(smooth_rows(above_ref, mid_ref, below_ref)):
        local_ref[m] = value

    def emit(level, value):
        analysis_ref[level] = before_ref[level] + value
        out_ref[level] = residual_ref[level] - RELAX * value

    increments(place_ref, member_refs, local_ref, residual_ref.shape[0], emit)


def per_device(residual_in, members, wind_x, wind_y):
    levels, rows, cols = residual_in.shape
    tiles = lax.axis_size("tile")
    parts = lax.axis_size("member")
    place = jnp.stack([lax.axis_index("tile"), jnp.int32(tiles), lax.axis_index("member"), jnp.int32(parts)])
    count = members.shape[0] * parts
    groups = levels // GROUP

    def shape(*dims, kind=F32):
        return jax.ShapeDtypeStruct(dims, kind)

    def both(*dims):
        return shape(*dims), shape(*dims, kind=BF16)

    def turned(x, step):
        return lax.ppermute(x, "member", [(i, (i + step) % parts) for i in range(parts)])

    def smoothed(wide, thin, planes):
        wide, thin = call(
            columns_body, both(planes, rows, cols), shift(thin, "member", 1), wide, shift(thin, "member", -1)
        )
        return shift(thin, "tile", 1), wide, shift(thin, "tile", -1)

    like = shape(levels, rows, cols)
    halo = shape((levels + groups) // 2, SUB, LANES)
    thin_halo = shape((levels + groups) // 4, 2 * SUB, LANES, kind=BF16)
    wide_halo = [pltpu.VMEM(halo.shape, F32)] * 2
    packed = shape(groups, rows, LANES)
    wind_x, wind_y = (jnp.broadcast_to(w[:, None], (levels, LANES)) for w in (wind_x, wind_y))

    first, last = call(columns_edge_body, (packed, packed), residual_in)
    left, right = shift(last, "member", 1), shift(first, "member", -1)
    blocks, left, right = lax.optimization_barrier((split_columns(place, members, parts), left, right))
    blocks = [turned(x, r) if r else x for r, x in enumerate(blocks)]
    around, top, bottom = call(rows_body, (packed, halo, halo), residual_in, left, right)
    members, around = lax.optimization_barrier((members, around))
    sides = side_columns(place, members, parts)
    above, below = shift(bottom, "tile", 1), shift(top, "tile", -1)
    grad = call(
        first_model_body, like,
        place, wind_x, wind_y, residual_in, around, above, below, in_specs=[SMEM] + [VMEM] * 6,
    )
    grad, sides = lax.optimization_barrier((grad, sides))
    grad, sides = lax.optimization_barrier((grad, [turned(x, r) if r else x for r, x in enumerate(sides)]))
    wide, thin = call(
        project_body, both(count, rows, cols), place, grad, *blocks, in_specs=[SMEM] + [VMEM] * (1 + parts)
    )

    analysis, residual, beside, top, bottom = call(
        functools.partial(update_body, parts), (like, like, packed, thin_halo, thin_halo),
        place, residual_in, around, *smoothed(wide, thin, 2 * count), *blocks, *sides,
        in_specs=[SMEM] + [VMEM] * (5 + 2 * parts),
        scratch=[pltpu.VMEM((2 * count, rows, cols), F32)] + wide_halo,
    )
    above, below = shift(bottom, "tile", 1), shift(top, "tile", -1)
    wide, thin = call(
        second_model_body, both(count, rows, cols),
        place, wind_x, wind_y, residual, beside, above, below, *blocks,
        in_specs=[SMEM] + [VMEM] * (6 + parts), scratch=[pltpu.VMEM((levels, rows, cols), F32)] + wide_halo,
    )
    return call(
        functools.partial(final_body, parts), (like, like),
        place, residual, analysis, *smoothed(wide, thin, count), *blocks,
        in_specs=[SMEM] + [VMEM] * (5 + parts), scratch=[pltpu.VMEM((count, rows, cols), F32)],
    )


def solution(mesh):
    return jax.shard_map(
        per_device,
        mesh=mesh,
        in_specs=(P(None, "tile", "member"), P("member", None, "tile", None), P(), P()),
        out_specs=(P(None, "tile", "member"), P(None, "tile", "member")),
        check_vma=False,
    )
```

time: 129 us -> 118 us (0.915)
  Pallas kernels: 26.1 us -> 22.2 us
  local copies, waits for them, and re-layouts: 6.55 us -> 2.78 us
  starting transfers between devices: 48.9 us -> 46.1 us
    ppermute x14, waiting for transfers between devices: 45.7 us -> 14.8 us  [shift(): return lax.ppermute(x, axis, pairs)]
    ppermute x3 -> x6, waiting for transfers between devices: 0.01 us -> 30.5 us  [turned(): lax.ppermute(x, 'member', [(i, (i + step) % parts) for i in range(parts)])]
    all_to_all x1 -> x0, starting transfers between devices: 5.34 us -> none  [per_device(): lax.all_to_all(soon, 'member', split_axis=0, concat_axis=0, tiled=True)]
    pallas_call x11, Pallas kernels: 26.1 us -> 22.2 us  [call(): pl.pallas_call(body, out_shape=out_shape, in_specs=in_specs or [VMEM] * l...]
    unnamed x32 -> x12, local copies, waits for them, and re-layouts: 6.41 us -> 2.64 us
    ppermute x3 -> x6, starting transfers between devices: 3.63 us -> 5.98 us  [turned(): lax.ppermute(x, 'member', [(i, (i + step) % parts) for i in range(parts)])]
  transfers between devices with their start and end apart: 18 -> 20, of which waited for: 9 -> 8; matrix products, arithmetic and copies ran while one was open for 0% -> 0% of each run, Pallas kernels for 10% -> 9%
where the time goes in v2:
time: 118 us; the launch traced here: 117 us
  starting transfers between devices  46.1 us (39%)
  waiting for transfers between devices  45.2 us (38%)
  Pallas kernels  22.2 us (19%)
  local copies, waits for them, and re-layouts  2.78 us (2%)
    ppermute x14, starting transfers between devices, shift(): return lax.ppermute(x, axis, pairs)  40.1 us
    ppermute x6, waiting for transfers between devices, turned(): lax.ppermute(x, 'member', [(i, (i + step) % parts) for i in range(parts)])  30.5 us
    pallas_call x11, Pallas kernels, call(): pl.pallas_call(body, out_shape=out_shape, in_specs=in_specs or [VMEM] * l...  22.2 us
    ppermute x14, waiting for transfers between devices, shift(): return lax.ppermute(x, axis, pairs)  14.8 us
    ppermute x6, starting transfers between devices, turned(): lax.ppermute(x, 'member', [(i, (i + step) % parts) for i in range(parts)])  5.98 us
    unnamed x12, local copies, waits for them, and re-layouts  2.64 us
  transfers between devices with their start and end apart: 20, of which 8 were waited for; matrix products, arithmetic and copies ran while one was open for 0% of the time, Pallas kernels for 9%

profile of v2, /device:TPU:20, one launch (start us, length us, event | category | flops | bytes accessed | tf_op | source)
XLA Modules:
  0.0 117.3 jit_solution(1869556542689301151)
XLA Ops:
  0.6 1.0 copy-done.2
  2.0 3.5 %collective-permute-start = (f32[4,16,128]{2,1,0:T(8,128)S(1)}, f32[4,16,128]{2,1,0:T(8,128)S(1)}, u32[]{:S(2)}, u32[]{:S(2)}) collective-permute-start(f32[4,16,128]{2,1,0:T(8,128)S(1)} %get-tuple-element.50), channel_id=1, source_target_pairs={{0,1},{1,2},{2,3},{4,5},{5,6},{6,7},{8,9},{9,10},{10,11},{12,13},{... | collective-permute-start | bytes 98312 | tf_op jit(solution)/shard_map/ppermute | solution.py:136
  5.5 2.4 %collective-permute-start.1 = (f32[4,16,128]{2,1,0:T(8,128)S(1)}, f32[4,16,128]{2,1,0:T(8,128)S(1)}, u32[]{:S(2)}, u32[]{:S(2)}) collective-permute-start(f32[4,16,128]{2,1,0:T(8,128)S(1)} %get-tuple-element.51), channel_id=1, source_target_pairs={{1,0},{2,1},{3,2},{5,4},{6,5},{7,6},{9,8},{10,9},{11,10},{13,12},{... | collective-permute-start | bytes 98312 | tf_op jit(solution)/shard_map/ppermute | solution.py:136
  8.0 1.6 %copy-done = bf16[2,64,16,512]{3,2,1,0:T(8,128)(2,1)S(1)} copy-done((bf16[2,64,16,512]{3,2,1,0:T(8,128)(2,1)S(1)}, bf16[2,64,16,512]{3,2,1,0:T(8,128)(2,1)}, u32[]{:S(2)}) %copy-start) | copy-done | bytes 2097176
  12.1 1.1 collective-permute-start.8
  13.2 1.3 %collective-permute-start.9 = (bf16[2,64,16,128]{3,2,1,0:T(8,128)(2,1)S(1)}, bf16[2,64,16,128]{3,2,1,0:T(8,128)(2,1)S(1)}, u32[]{:S(2)}, u32[]{:S(2)}) collective-permute-start(bf16[2,64,16,128]{3,2,1,0:T(8,128)(2,1)S(1)} %get-tuple-element.72), channel_id=1, source_target_pairs={{0,3},{1,0},{2,1},{3,2},{4,7},{5,4},{6,5},{7,6},{8,11},{9,8},{10,9... | collective-permute-start | bytes 1572872 | tf_op jit(solution)/shard_map/ppermute | solution.py:383
  14.6 1.9 %collective-permute-start.2 = (f32[34,8,128]{2,1,0:T(8,128)S(1)}, f32[34,8,128]{2,1,0:T(8,128)S(1)}, u32[]{:S(2)}, u32[]{:S(2)}) collective-permute-start(f32[34,8,128]{2,1,0:T(8,128)S(1)} %get-tuple-element.56), channel_id=1, source_target_pairs={{0,4},{4,8},{8,12},{12,16},{16,20},{20,24},{24,28},{1,5},{5,9},{9,... | collective-permute-start | bytes 417800 | tf_op jit(solution)/shard_map/ppermute | solution.py:136
  16.5 4.5 %collective-permute-start.3 = (f32[34,8,128]{2,1,0:T(8,128)S(1)}, f32[34,8,128]{2,1,0:T(8,128)S(1)}, u32[]{:S(2)}, u32[]{:S(2)}) collective-permute-start(f32[34,8,128]{2,1,0:T(8,128)S(1)} %get-tuple-element.57), channel_id=1, source_target_pairs={{4,0},{8,4},{12,8},{16,12},{20,16},{24,20},{28,24},{5,1},{9,5},{13... | collective-permute-start | bytes 417800 | tf_op jit(solution)/shard_map/ppermute | solution.py:136
  21.1 4.0 %shard_map.63 = (bf16[2,4,16,128]{3,2,1,0:T(8,128)(2,1)S(1)}, bf16[2,4,16,128]{3,2,1,0:T(8,128)(2,1)S(1)}, bf16[2,4,16,128]{3,2,1,0:T(8,128)(2,1)S(1)}, bf16[2,4,16,128]{3,2,1,0:T(8,128)(2,1)S(1)}) custom-call(s32[4]{0:T(128)S(1)} %pad_add_fusion.place_ref, bf16[2,64,16,512]{3,2,1,0:T(8,128)(2,1)S(1)} %copy-done.1), custom_call_target="tpu_custom_call" | custom-call | tf_op jit(solution)/shard_map/pallas_call | solution.py:28
  25.2 5.3 %shard_map.62.grad_ref = f32[64,16,128]{2,1,0:T(8,128)S(1)} custom-call(s32[4]{0:T(128)S(1)} %pad_add_fusion.place_ref, f32[64,128]{1,0:T(8,128)S(1)} %broadcast_in_dim.4.wx_ref, f32[64,128]{1,0:T(8,128)S(1)} %broadcast_in_dim.5.wy_ref, f32[64,16,128]{2,1,0:T(8,128)S(1)} %copy-done.3, f32[4,16,128]{2,1,0:T(8,128)S(1)} %get-tuple-element.55.beside_ref.around_ref, ...), custom_call_target="tpu_custom_call" | custom-call | tf_op jit(solution)/shard_map/pallas_call | solution.py:28
  31.3 2.0 %collective-permute-start.5 = (bf16[2,4,16,128]{3,2,1,0:T(8,128)(2,1)S(1)}, bf16[2,4,16,128]{3,2,1,0:T(8,128)(2,1)S(1)}, u32[]{:S(2)}, u32[]{:S(2)}) collective-permute-start(bf16[2,4,16,128]{3,2,1,0:T(8,128)(2,1)S(1)} %get-tuple-element.66), channel_id=1, source_target_pairs={{0,2},{1,3},{2,0},{3,1},{4,6},{5,7},{6,4},{7,5},{8,10},{9,11},{10,... | collective-permute-start | bytes 98312 | tf_op jit(solution)/shard_map/ppermute | solution.py:383
  33.3 26.6 %collective-permute-done.4.refs_5_ = bf16[2,4,16,128]{3,2,1,0:T(8,128)(2,1)S(1)} collective-permute-done((bf16[2,4,16,128]{3,2,1,0:T(8,128)(2,1)S(1)}, bf16[2,4,16,128]{3,2,1,0:T(8,128)(2,1)S(1)}, u32[]{:S(2)}, u32[]{:S(2)}) %collective-permute-start.4) | collective-permute-done | bytes 32800 | tf_op jit(solution)/shard_map/ppermute | solution.py:383
  59.8 3.9 %collective-permute-done.6.refs_7_ = bf16[2,4,16,128]{3,2,1,0:T(8,128)(2,1)S(1)} collective-permute-done((bf16[2,4,16,128]{3,2,1,0:T(8,128)(2,1)S(1)}, bf16[2,4,16,128]{3,2,1,0:T(8,128)(2,1)S(1)}, u32[]{:S(2)}, u32[]{:S(2)}) %collective-permute-start.6) | collective-permute-done | bytes 32800 | tf_op jit(solution)/shard_map/ppermute | solution.py:383
  63.7 1.2 %shard_map.64 = (f32[8,16,128]{2,1,0:T(8,128)S(1)}, bf16[8,16,128]{2,1,0:T(8,128)(2,1)S(1)}) custom-call(s32[4]{0:T(128)S(1)} %pad_add_fusion.place_ref, f32[64,16,128]{2,1,0:T(8,128)S(1)} %shard_map.62.grad_ref, bf16[2,64,16,128]{3,2,1,0:T(8,128)(2,1)S(1)} %get-tuple-element.69.refs_0_, bf16[2,64,16,128]{3,2,1,0:T(8,128)(2,1)S(1)} %collective-permute-done.7.refs_1_, ...), custom_call_target="tpu_custom_call" | custom-call | tf_op jit(solution)/shard_map/pallas_call | solution.py:28
  64.9 1.9 %collective-permute-start.11 = (bf16[8,16,128]{2,1,0:T(8,128)(2,1)S(1)}, bf16[8,16,128]{2,1,0:T(8,128)(2,1)S(1)}, u32[]{:S(2)}, u32[]{:S(2)}) collective-permute-start(bf16[8,16,128]{2,1,0:T(8,128)(2,1)S(1)} %get-tuple-element.73), channel_id=1, source_target_pairs={{1,0},{2,1},{3,2},{5,4},{6,5},{7,6},{9,8},{10,9},{11,10},{13,12},{... | collective-permute-start | bytes 98312 | tf_op jit(solution)/shard_map/ppermute | solution.py:136
  66.9 3.9 %collective-permute-start.10 = (bf16[8,16,128]{2,1,0:T(8,128)(2,1)S(1)}, bf16[8,16,128]{2,1,0:T(8,128)(2,1)S(1)}, u32[]{:S(2)}, u32[]{:S(2)}) collective-permute-start(bf16[8,16,128]{2,1,0:T(8,128)(2,1)S(1)} %get-tuple-element.73), channel_id=1, source_target_pairs={{0,1},{1,2},{2,3},{4,5},{5,6},{6,7},{8,9},{9,10},{10,11},{12,13},{... | collective-permute-start | bytes 98312 | tf_op jit(solution)/shard_map/ppermute | solution.py:136
  70.8 1.9 %collective-permute-done.10.left_ref = bf16[8,16,128]{2,1,0:T(8,128)(2,1)S(1)} collective-permute-done((bf16[8,16,128]{2,1,0:T(8,128)(2,1)S(1)}, bf16[8,16,128]{2,1,0:T(8,128)(2,1)S(1)}, u32[]{:S(2)}, u32[]{:S(2)}) %collective-permute-start.10) | collective-permute-done | bytes 32800 | tf_op jit(solution)/shard_map/ppermute | solution.py:136
  73.1 1.9 %collective-permute-start.13 = (bf16[16,16,128]{2,1,0:T(8,128)(2,1)S(1)}, bf16[16,16,128]{2,1,0:T(8,128)(2,1)S(1)}, u32[]{:S(2)}, u32[]{:S(2)}) collective-permute-start(bf16[16,16,128]{2,1,0:T(8,128)(2,1)S(1)} %get-tuple-element.75), channel_id=1, source_target_pairs={{4,0},{8,4},{12,8},{16,12},{20,16},{24,20},{28,24},{5,1},{9,5},{13... | collective-permute-start | bytes 196616 | tf_op jit(solution)/shard_map/ppermute | solution.py:136
  75.0 2.4 %collective-permute-start.12 = (bf16[16,16,128]{2,1,0:T(8,128)(2,1)S(1)}, bf16[16,16,128]{2,1,0:T(8,128)(2,1)S(1)}, u32[]{:S(2)}, u32[]{:S(2)}) collective-permute-start(bf16[16,16,128]{2,1,0:T(8,128)(2,1)S(1)} %get-tuple-element.75), channel_id=1, source_target_pairs={{0,4},{4,8},{8,12},{12,16},{16,20},{20,24},{24,28},{1,5},{5,9},{9,... | collective-permute-start | bytes 196616 | tf_op jit(solution)/shard_map/ppermute | solution.py:136
  77.4 4.1 %collective-permute-done.12.above_ref = bf16[16,16,128]{2,1,0:T(8,128)(2,1)S(1)} collective-permute-done((bf16[16,16,128]{2,1,0:T(8,128)(2,1)S(1)}, bf16[16,16,128]{2,1,0:T(8,128)(2,1)S(1)}, u32[]{:S(2)}, u32[]{:S(2)}) %collective-permute-start.12) | collective-permute-done | bytes 65568 | tf_op jit(solution)/shard_map/ppermute | solution.py:136
  81.5 1.5 %shard_map.66 = (f32[64,16,128]{2,1,0:T(8,128)S(1)}, f32[64,16,128]{2,1,0:T(8,128)S(1)}, f32[4,16,128]{2,1,0:T(8,128)S(1)}, bf16[17,16,128]{2,1,0:T(8,128)(2,1)S(1)}, bf16[17,16,128]{2,1,0:T(8,128)(2,1)S(1)}) custom-call(s32[4]{0:T(128)S(1)} %pad_add_fusion.place_ref, f32[64,16,128]{2,1,0:T(8,128)S(1)} %copy-done.3, ...), custom_call_target="tpu_custom_call" | custom-call | tf_op jit(solution)/shard_map/pallas_call | solution.py:28
  83.0 1.9 %collective-permute-start.14 = (bf16[17,16,128]{2,1,0:T(8,128)(2,1)S(1)}, bf16[17,16,128]{2,1,0:T(8,128)(2,1)S(1)}, u32[]{:S(2)}, u32[]{:S(2)}) collective-permute-start(bf16[17,16,128]{2,1,0:T(8,128)(2,1)S(1)} %get-tuple-element.84), channel_id=1, source_target_pairs={{0,4},{4,8},{8,12},{12,16},{16,20},{20,24},{24,28},{1,5},{5,9},{9,... | collective-permute-start | bytes 208904 | tf_op jit(solution)/shard_map/ppermute | solution.py:136
  84.9 4.5 %collective-permute-start.15 = (bf16[17,16,128]{2,1,0:T(8,128)(2,1)S(1)}, bf16[17,16,128]{2,1,0:T(8,128)(2,1)S(1)}, u32[]{:S(2)}, u32[]{:S(2)}) collective-permute-start(bf16[17,16,128]{2,1,0:T(8,128)(2,1)S(1)} %get-tuple-element.85), channel_id=1, source_target_pairs={{4,0},{8,4},{12,8},{16,12},{20,16},{24,20},{28,24},{5,1},{9,5},{13... | collective-permute-start | bytes 208904 | tf_op jit(solution)/shard_map/ppermute | solution.py:136
  89.5 1.9 %collective-permute-done.15.below_thin_ref = bf16[17,16,128]{2,1,0:T(8,128)(2,1)S(1)} collective-permute-done((bf16[17,16,128]{2,1,0:T(8,128)(2,1)S(1)}, bf16[17,16,128]{2,1,0:T(8,128)(2,1)S(1)}, u32[]{:S(2)}, u32[]{:S(2)}) %collective-permute-start.15) | collective-permute-done | bytes 69664 | tf_op jit(solution)/shard_map/ppermute | solution.py:136
  91.4 5.9 %shard_map.67 = (f32[8,16,128]{2,1,0:T(8,128)S(1)}, bf16[8,16,128]{2,1,0:T(8,128)(2,1)S(1)}) custom-call(s32[4]{0:T(128)S(1)} %pad_add_fusion.place_ref, f32[64,128]{1,0:T(8,128)S(1)} %broadcast_in_dim.4.wx_ref, f32[64,128]{1,0:T(8,128)S(1)} %broadcast_in_dim.5.wy_ref, f32[64,16,128]{2,1,0:T(8,128)S(1)} %get-tuple-element.81.x_ref.residual_ref, ...), custom_call_target="tpu_custom_call" | custom-call | tf_op jit(solution)/shard_map/pallas_call | solution.py:28
  97.3 1.9 %collective-permute-start.17 = (bf16[8,16,128]{2,1,0:T(8,128)(2,1)S(1)}, bf16[8,16,128]{2,1,0:T(8,128)(2,1)S(1)}, u32[]{:S(2)}, u32[]{:S(2)}) collective-permute-start(bf16[8,16,128]{2,1,0:T(8,128)(2,1)S(1)} %get-tuple-element.86), channel_id=1, source_target_pairs={{1,0},{2,1},{3,2},{5,4},{6,5},{7,6},{9,8},{10,9},{11,10},{13,12},{... | collective-permute-start | bytes 98312 | tf_op jit(solution)/shard_map/ppermute | solution.py:136
  99.3 3.9 %collective-permute-start.16 = (bf16[8,16,128]{2,1,0:T(8,128)(2,1)S(1)}, bf16[8,16,128]{2,1,0:T(8,128)(2,1)S(1)}, u32[]{:S(2)}, u32[]{:S(2)}) collective-permute-start(bf16[8,16,128]{2,1,0:T(8,128)(2,1)S(1)} %get-tuple-element.86), channel_id=1, source_target_pairs={{0,1},{1,2},{2,3},{4,5},{5,6},{6,7},{8,9},{9,10},{10,11},{12,13},{... | collective-permute-start | bytes 98312 | tf_op jit(solution)/shard_map/ppermute | solution.py:136
  103.2 1.9 %collective-permute-done.16.left_ref = bf16[8,16,128]{2,1,0:T(8,128)(2,1)S(1)} collective-permute-done((bf16[8,16,128]{2,1,0:T(8,128)(2,1)S(1)}, bf16[8,16,128]{2,1,0:T(8,128)(2,1)S(1)}, u32[]{:S(2)}, u32[]{:S(2)}) %collective-permute-start.16) | collective-permute-done | bytes 32800 | tf_op jit(solution)/shard_map/ppermute | solution.py:136
  105.3 3.4 %collective-permute-start.19 = (bf16[8,16,128]{2,1,0:T(8,128)(2,1)S(1)}, bf16[8,16,128]{2,1,0:T(8,128)(2,1)S(1)}, u32[]{:S(2)}, u32[]{:S(2)}) collective-permute-start(bf16[8,16,128]{2,1,0:T(8,128)(2,1)S(1)} %get-tuple-element.88), channel_id=1, source_target_pairs={{4,0},{8,4},{12,8},{16,12},{20,16},{24,20},{28,24},{5,1},{9,5},{13... | collective-permute-start | bytes 98312 | tf_op jit(solution)/shard_map/ppermute | solution.py:136
  108.8 1.9 %collective-permute-start.18 = (bf16[8,16,128]{2,1,0:T(8,128)(2,1)S(1)}, bf16[8,16,128]{2,1,0:T(8,128)(2,1)S(1)}, u32[]{:S(2)}, u32[]{:S(2)}) collective-permute-start(bf16[8,16,128]{2,1,0:T(8,128)(2,1)S(1)} %get-tuple-element.88), channel_id=1, source_target_pairs={{0,4},{4,8},{8,12},{12,16},{16,20},{20,24},{24,28},{1,5},{5,9},{9,... | collective-permute-start | bytes 98312 | tf_op jit(solution)/shard_map/ppermute | solution.py:136
  110.7 4.2 %collective-permute-done.18.above_ref = bf16[8,16,128]{2,1,0:T(8,128)(2,1)S(1)} collective-permute-done((bf16[8,16,128]{2,1,0:T(8,128)(2,1)S(1)}, bf16[8,16,128]{2,1,0:T(8,128)(2,1)S(1)}, u32[]{:S(2)}, u32[]{:S(2)}) %collective-permute-start.18) | collective-permute-done | bytes 32800 | tf_op jit(solution)/shard_map/ppermute | solution.py:136
  114.9 2.4 %shard_map.69 = (f32[64,16,128]{2,1,0:T(8,128)}, f32[64,16,128]{2,1,0:T(8,128)}) custom-call(s32[4]{0:T(128)S(1)} %pad_add_fusion.place_ref, f32[64,16,128]{2,1,0:T(8,128)S(1)} %get-tuple-element.81.x_ref.residual_ref, f32[64,16,128]{2,1,0:T(8,128)S(1)} %get-tuple-element.82.before_ref, bf16[8,16,128]{2,1,0:T(8,128)(2,1)S(1)} %collective-permute-done.18.above_ref, ...), custom_call_target="tpu_custom_call" | custom-call | tf_op jit(solution)/shard_map/pallas_call | solution.py:28
  (34 shorter events, 4.6 us)
Async XLA Ops:
  0.6 1.0 copy-start.2
  1.7 12.9 %copy-start.3 = (f32[64,16,128]{2,1,0:T(8,128)S(1)}, f32[64,16,128]{2,1,0:T(8,128)}, u32[]{:S(2)}) copy-start(f32[64,16,128]{2,1,0:T(8,128)} %residual_ref.1) | copy-start | bytes 1572868
  2.0 8.5 %collective-permute-start = (f32[4,16,128]{2,1,0:T(8,128)S(1)}, f32[4,16,128]{2,1,0:T(8,128)S(1)}, u32[]{:S(2)}, u32[]{:S(2)}) collective-permute-start(f32[4,16,128]{2,1,0:T(8,128)S(1)} %get-tuple-element.50), channel_id=1, source_target_pairs={{0,1},{1,2},{2,3},{4,5},{5,6},{6,7},{8,9},{9,10},{10,11},{12,13},{... | collective-permute-start | bytes 98312 | tf_op jit(solution)/shard_map/ppermute | solution.py:136
  5.5 5.8 %collective-permute-start.1 = (f32[4,16,128]{2,1,0:T(8,128)S(1)}, f32[4,16,128]{2,1,0:T(8,128)S(1)}, u32[]{:S(2)}, u32[]{:S(2)}) collective-permute-start(f32[4,16,128]{2,1,0:T(8,128)S(1)} %get-tuple-element.51), channel_id=1, source_target_pairs={{1,0},{2,1},{3,2},{5,4},{6,5},{7,6},{9,8},{10,9},{11,10},{13,12},{... | collective-permute-start | bytes 98312 | tf_op jit(solution)/shard_map/ppermute | solution.py:136
  7.9 1.6 %copy-start = (bf16[2,64,16,512]{3,2,1,0:T(8,128)(2,1)S(1)}, bf16[2,64,16,512]{3,2,1,0:T(8,128)(2,1)}, u32[]{:S(2)}) copy-start(bf16[2,64,16,512]{3,2,1,0:T(8,128)(2,1)} %in_ref.2) | copy-start | bytes 6291460
  9.5 11.5 %copy-start.1 = (bf16[2,64,16,512]{3,2,1,0:T(8,128)(2,1)S(1)}, bf16[2,64,16,512]{3,2,1,0:T(8,128)(2,1)}, u32[]{:S(2)}) copy-start(bf16[2,64,16,512]{3,2,1,0:T(8,128)(2,1)} %in_ref.2) | copy-start | bytes 6291460
  9.5 15.5 %copy-start.4 = (f32[64]{0:T(128)S(1)}, f32[64]{0:T(128)}, u32[]{:S(2)}) copy-start(f32[64]{0:T(128)} %param.6) | copy-start | bytes 772
  9.5 15.6 %copy-start.5 = (f32[64]{0:T(128)S(1)}, f32[64]{0:T(128)}, u32[]{:S(2)}) copy-start(f32[64]{0:T(128)} %param.7) | copy-start | bytes 772
  11.3 52.4 %collective-permute-start.7 = (bf16[2,64,16,128]{3,2,1,0:T(8,128)(2,1)S(1)}, bf16[2,64,16,128]{3,2,1,0:T(8,128)(2,1)S(1)}, u32[]{:S(2)}, u32[]{:S(2)}) collective-permute-start(bf16[2,64,16,128]{3,2,1,0:T(8,128)(2,1)S(1)} %get-tuple-element.70), channel_id=1, source_target_pairs={{0,1},{1,2},{2,3},{3,0},{4,5},{5,6},{6,7},{7,4},{8,9},{9,10},{10,1... | collective-permute-start | bytes 1572872 | tf_op jit(solution)/shard_map/ppermute | solution.py:383
  12.1 51.6 %collective-permute-start.8 = (bf16[2,64,16,128]{3,2,1,0:T(8,128)(2,1)S(1)}, bf16[2,64,16,128]{3,2,1,0:T(8,128)(2,1)S(1)}, u32[]{:S(2)}, u32[]{:S(2)}) collective-permute-start(bf16[2,64,16,128]{3,2,1,0:T(8,128)(2,1)S(1)} %get-tuple-element.71), channel_id=1, source_target_pairs={{0,2},{1,3},{2,0},{3,1},{4,6},{5,7},{6,4},{7,5},{8,10},{9,11},{10,... | collective-permute-start | bytes 1572872 | tf_op jit(solution)/shard_map/ppermute | solution.py:383
  13.2 50.5 %collective-permute-start.9 = (bf16[2,64,16,128]{3,2,1,0:T(8,128)(2,1)S(1)}, bf16[2,64,16,128]{3,2,1,0:T(8,128)(2,1)S(1)}, u32[]{:S(2)}, u32[]{:S(2)}) collective-permute-start(bf16[2,64,16,128]{3,2,1,0:T(8,128)(2,1)S(1)} %get-tuple-element.72), channel_id=1, source_target_pairs={{0,3},{1,0},{2,1},{3,2},{4,7},{5,4},{6,5},{7,6},{8,11},{9,8},{10,9... | collective-permute-start | bytes 1572872 | tf_op jit(solution)/shard_map/ppermute | solution.py:383
  14.6 10.5 %collective-permute-start.2 = (f32[34,8,128]{2,1,0:T(8,128)S(1)}, f32[34,8,128]{2,1,0:T(8,128)S(1)}, u32[]{:S(2)}, u32[]{:S(2)}) collective-permute-start(f32[34,8,128]{2,1,0:T(8,128)S(1)} %get-tuple-element.56), channel_id=1, source_target_pairs={{0,4},{4,8},{8,12},{12,16},{16,20},{20,24},{24,28},{1,5},{5,9},{9,... | collective-permute-start | bytes 417800 | tf_op jit(solution)/shard_map/ppermute | solution.py:136
  16.5 8.5 %collective-permute-start.3 = (f32[34,8,128]{2,1,0:T(8,128)S(1)}, f32[34,8,128]{2,1,0:T(8,128)S(1)}, u32[]{:S(2)}, u32[]{:S(2)}) collective-permute-start(f32[34,8,128]{2,1,0:T(8,128)S(1)} %get-tuple-element.57), channel_id=1, source_target_pairs={{4,0},{8,4},{12,8},{16,12},{20,16},{24,20},{28,24},{5,1},{9,5},{13... | collective-permute-start | bytes 417800 | tf_op jit(solution)/shard_map/ppermute | solution.py:136
  30.5 29.3 %collective-permute-start.4 = (bf16[2,4,16,128]{3,2,1,0:T(8,128)(2,1)S(1)}, bf16[2,4,16,128]{3,2,1,0:T(8,128)(2,1)S(1)}, u32[]{:S(2)}, u32[]{:S(2)}) collective-permute-start(bf16[2,4,16,128]{3,2,1,0:T(8,128)(2,1)S(1)} %get-tuple-element.65), channel_id=1, source_target_pairs={{0,1},{1,2},{2,3},{3,0},{4,5},{5,6},{6,7},{7,4},{8,9},{9,10},{10,1... | collective-permute-start | bytes 98312 | tf_op jit(solution)/shard_map/ppermute | solution.py:383
  31.3 28.6 %collective-permute-start.5 = (bf16[2,4,16,128]{3,2,1,0:T(8,128)(2,1)S(1)}, bf16[2,4,16,128]{3,2,1,0:T(8,128)(2,1)S(1)}, u32[]{:S(2)}, u32[]{:S(2)}) collective-permute-start(bf16[2,4,16,128]{3,2,1,0:T(8,128)(2,1)S(1)} %get-tuple-element.66), channel_id=1, source_target_pairs={{0,2},{1,3},{2,0},{3,1},{4,6},{5,7},{6,4},{7,5},{8,10},{9,11},{10,... | collective-permute-start | bytes 98312 | tf_op jit(solution)/shard_map/ppermute | solution.py:383
  59.8 3.9 %collective-permute-start.6 = (bf16[2,4,16,128]{3,2,1,0:T(8,128)(2,1)S(1)}, bf16[2,4,16,128]{3,2,1,0:T(8,128)(2,1)S(1)}, u32[]{:S(2)}, u32[]{:S(2)}) collective-permute-start(bf16[2,4,16,128]{3,2,1,0:T(8,128)(2,1)S(1)} %get-tuple-element.67), channel_id=1, source_target_pairs={{0,3},{1,0},{2,1},{3,2},{4,7},{5,4},{6,5},{7,6},{8,11},{9,8},{10,9... | collective-permute-start | bytes 98312 | tf_op jit(solution)/shard_map/ppermute | solution.py:383
  64.9 5.9 %collective-permute-start.11 = (bf16[8,16,128]{2,1,0:T(8,128)(2,1)S(1)}, bf16[8,16,128]{2,1,0:T(8,128)(2,1)S(1)}, u32[]{:S(2)}, u32[]{:S(2)}) collective-permute-start(bf16[8,16,128]{2,1,0:T(8,128)(2,1)S(1)} %get-tuple-element.73), channel_id=1, source_target_pairs={{1,0},{2,1},{3,2},{5,4},{6,5},{7,6},{9,8},{10,9},{11,10},{13,12},{... | collective-permute-start | bytes 98312 | tf_op jit(solution)/shard_map/ppermute | solution.py:136
  66.9 5.8 %collective-permute-start.10 = (bf16[8,16,128]{2,1,0:T(8,128)(2,1)S(1)}, bf16[8,16,128]{2,1,0:T(8,128)(2,1)S(1)}, u32[]{:S(2)}, u32[]{:S(2)}) collective-permute-start(bf16[8,16,128]{2,1,0:T(8,128)(2,1)S(1)} %get-tuple-element.73), channel_id=1, source_target_pairs={{0,1},{1,2},{2,3},{4,5},{5,6},{6,7},{8,9},{9,10},{10,11},{12,13},{... | collective-permute-start | bytes 98312 | tf_op jit(solution)/shard_map/ppermute | solution.py:136
  73.1 4.3 %collective-permute-start.13 = (bf16[16,16,128]{2,1,0:T(8,128)(2,1)S(1)}, bf16[16,16,128]{2,1,0:T(8,128)(2,1)S(1)}, u32[]{:S(2)}, u32[]{:S(2)}) collective-permute-start(bf16[16,16,128]{2,1,0:T(8,128)(2,1)S(1)} %get-tuple-element.75), channel_id=1, source_target_pairs={{4,0},{8,4},{12,8},{16,12},{20,16},{24,20},{28,24},{5,1},{9,5},{13... | collective-permute-start | bytes 196616 | tf_op jit(solution)/shard_map/ppermute | solution.py:136
  75.0 6.5 %collective-permute-start.12 = (bf16[16,16,128]{2,1,0:T(8,128)(2,1)S(1)}, bf16[16,16,128]{2,1,0:T(8,128)(2,1)S(1)}, u32[]{:S(2)}, u32[]{:S(2)}) collective-permute-start(bf16[16,16,128]{2,1,0:T(8,128)(2,1)S(1)} %get-tuple-element.75), channel_id=1, source_target_pairs={{0,4},{4,8},{8,12},{12,16},{16,20},{20,24},{24,28},{1,5},{5,9},{9,... | collective-permute-start | bytes 196616 | tf_op jit(solution)/shard_map/ppermute | solution.py:136
  83.0 6.5 %collective-permute-start.14 = (bf16[17,16,128]{2,1,0:T(8,128)(2,1)S(1)}, bf16[17,16,128]{2,1,0:T(8,128)(2,1)S(1)}, u32[]{:S(2)}, u32[]{:S(2)}) collective-permute-start(bf16[17,16,128]{2,1,0:T(8,128)(2,1)S(1)} %get-tuple-element.84), channel_id=1, source_target_pairs={{0,4},{4,8},{8,12},{12,16},{16,20},{20,24},{24,28},{1,5},{5,9},{9,... | collective-permute-start | bytes 208904 | tf_op jit(solution)/shard_map/ppermute | solution.py:136
  84.9 6.5 %collective-permute-start.15 = (bf16[17,16,128]{2,1,0:T(8,128)(2,1)S(1)}, bf16[17,16,128]{2,1,0:T(8,128)(2,1)S(1)}, u32[]{:S(2)}, u32[]{:S(2)}) collective-permute-start(bf16[17,16,128]{2,1,0:T(8,128)(2,1)S(1)} %get-tuple-element.85), channel_id=1, source_target_pairs={{4,0},{8,4},{12,8},{16,12},{20,16},{24,20},{28,24},{5,1},{9,5},{13... | collective-permute-start | bytes 208904 | tf_op jit(solution)/shard_map/ppermute | solution.py:136
  97.3 5.9 %collective-permute-start.17 = (bf16[8,16,128]{2,1,0:T(8,128)(2,1)S(1)}, bf16[8,16,128]{2,1,0:T(8,128)(2,1)S(1)}, u32[]{:S(2)}, u32[]{:S(2)}) collective-permute-start(bf16[8,16,128]{2,1,0:T(8,128)(2,1)S(1)} %get-tuple-element.86), channel_id=1, source_target_pairs={{1,0},{2,1},{3,2},{5,4},{6,5},{7,6},{9,8},{10,9},{11,10},{13,12},{... | collective-permute-start | bytes 98312 | tf_op jit(solution)/shard_map/ppermute | solution.py:136
  99.3 5.8 %collective-permute-start.16 = (bf16[8,16,128]{2,1,0:T(8,128)(2,1)S(1)}, bf16[8,16,128]{2,1,0:T(8,128)(2,1)S(1)}, u32[]{:S(2)}, u32[]{:S(2)}) collective-permute-start(bf16[8,16,128]{2,1,0:T(8,128)(2,1)S(1)} %get-tuple-element.86), channel_id=1, source_target_pairs={{0,1},{1,2},{2,3},{4,5},{5,6},{6,7},{8,9},{9,10},{10,11},{12,13},{... | collective-permute-start | bytes 98312 | tf_op jit(solution)/shard_map/ppermute | solution.py:136
  105.3 5.4 %collective-permute-start.19 = (bf16[8,16,128]{2,1,0:T(8,128)(2,1)S(1)}, bf16[8,16,128]{2,1,0:T(8,128)(2,1)S(1)}, u32[]{:S(2)}, u32[]{:S(2)}) collective-permute-start(bf16[8,16,128]{2,1,0:T(8,128)(2,1)S(1)} %get-tuple-element.88), channel_id=1, source_target_pairs={{4,0},{8,4},{12,8},{16,12},{20,16},{24,20},{28,24},{5,1},{9,5},{13... | collective-permute-start | bytes 98312 | tf_op jit(solution)/shard_map/ppermute | solution.py:136
  108.8 6.1 %collective-permute-start.18 = (bf16[8,16,128]{2,1,0:T(8,128)(2,1)S(1)}, bf16[8,16,128]{2,1,0:T(8,128)(2,1)S(1)}, u32[]{:S(2)}, u32[]{:S(2)}) collective-permute-start(bf16[8,16,128]{2,1,0:T(8,128)(2,1)S(1)} %get-tuple-element.88), channel_id=1, source_target_pairs={{0,4},{4,8},{8,12},{12,16},{16,20},{20,24},{24,28},{1,5},{5,9},{9,... | collective-permute-start | bytes 98312 | tf_op jit(solution)/shard_map/ppermute | solution.py:136
